TPU v7x, 512 devices: a whole 4x8x8 slice. The times are simulated.
512 devices in a mesh: lon: 32 (over y, x), lat: 16 (over z, core).
Axes of the slice: x: 4, y: 8, z: 8, core: 2. Of those that a mesh axis runs over, the one named last changes fastest.
Arguments:
- tendency: float32 [3, 16, 16, 32, 2304], P(None, None, 'lat', 'lon'), may hold values from -8 to 8
- state: float32 [16, 3, 2, 512, 512], P('lat', None, None, 'lon'), may hold values from -6 to 6
- stiffness: float32 [16], replicated, may hold values from 0.2 to 20
- damping: float32 [16], replicated, may hold values from 0.05 to 2
Outputs:
- new_state: float32 [16, 3, 2, 512, 512], P('lat', None, None, 'lon')
- new_fields: float32 [3, 16, 16, 32, 2304], P(None, None, 'lat', 'lon')
All inputs are finite; a program needn't handle non-finite values.
Results may differ from a plain program's by a relative error of at most 0.0044.
Values sent between devices are 32-bit elements; how exact they have to be, the bound alone decides.
A program may use at most 128 MiB of HBM per device.

v0:
```python
import functools
import math

import jax
import jax.numpy as jnp
import ml_dtypes
import numpy as np
from jax import lax
from jax.experimental import pallas as pl
from jax.experimental.pallas import tpu as pltpu
from jax.sharding import PartitionSpec as P

NLAT = 768
NLON = 1536
WAVES = 512
MODES = 16
LON = 32
LAT = 16
BLK = 48
MDEV = 16
GROUPS = 8
MSG_G = 27
MSG_C = 18
FR = 6
ROWS = 48
MESH = pl.DeviceIdType.MESH
F32 = jnp.float32
BF16 = jnp.bfloat16


def split_constant(table):
    high = table.astype(np.float32).astype(ml_dtypes.bfloat16)
    low = (table - high.astype(np.float64)).astype(np.float32).astype(ml_dtypes.bfloat16)
    return high, low


@functools.lru_cache(maxsize=None)
def fourier_constants():
    slot = np.arange(LON * 64)
    block, inner = slot // 64, slot % 64
    lon = block * BLK + inner
    valid = (inner < BLK)[:, None]
    wave = np.arange(WAVES)
    angle = 2.0 * np.pi / NLON * ((lon[:, None] * wave[None, :]) % NLON)
    cosine = np.where(valid, np.cos(angle), 0.0).reshape(-1, LON, MDEV)
    sine = np.where(valid, np.sin(angle), 0.0).reshape(-1, LON, MDEV)
    basis = np.stack([cosine, -sine], axis=2).reshape(LON * 64, 2 * WAVES)
    factor = np.where(wave == 0, 1.0, 2.0).reshape(LON, 1, MDEV) / WAVES
    factor = np.broadcast_to(factor, (LON, 2, MDEV)).reshape(2 * WAVES, 1)
    return split_constant(basis / NLON) + split_constant(factor * basis.T)


@functools.lru_cache(maxsize=None)
def start_constants():
    start = [
        (0.5 * math.log(m + 0.5) + 0.5 * math.lgamma(m + 0.5) - 0.5 * math.lgamma(m + 1.0) - 0.25 * math.log(math.pi))
        / math.log(2.0)
        for m in range(WAVES)
    ]
    return np.tile(np.array(start, np.float32).reshape(LON, MDEV), (1, GROUPS))


def lanes(shape):
    return lax.broadcasted_iota(jnp.int32, shape, len(shape) - 1)


def swap_groups(items):
    group = lanes(items[0].shape) // 16
    items = list(items)
    for step in (4, 2, 1):
        keep = (group & step) == 0
        for low in range(GROUPS):
            if low & step:
                continue
            high = low + step
            x, y = items[low], items[high]
            items[low] = jnp.where(keep, x, pltpu.roll(y, 16 * step, 1))
            items[high] = jnp.where(keep, pltpu.roll(x, 128 - 16 * step, 1), y)
    return items


def fold_rows(parts):
    row = lax.broadcasted_iota(jnp.int32, (8, 128), 0)
    upper = row < 4
    four = []
    for index in range(4):
        x, y = parts[index], parts[index + 4]
        four.append(jnp.where(upper, x, y) + pltpu.roll(jnp.where(upper, y, x), 4, 0))
    for step in (2, 1):
        keep = (row & step) == 0
        four = [
            jnp.where(
                keep,
                four[index] + pltpu.roll(four[index], 8 - step, 0),
                four[index + step] + pltpu.roll(four[index + step], step, 0),
            )
            for index in range(step)
        ]
    return four[0]


def split(x):
    high = x.astype(BF16)
    return high, (x - high.astype(F32)).astype(BF16)


def mirrored(south, a):
    return jnp.where(south, GROUPS - 1 - a, a)


def block_rows(index, size):
    return pl.ds(pl.multiple_of(index * size, size), size)


def gather_rows(t_ref, sb_ref):
    def body(d, _):
        c, h = d // 2, d % 2
        for f in range(3):
            sb_ref[pl.ds(d * MSG_G + f * 9, 9), :] = t_ref[pl.ds((f * MODES + c) * 18 + h * 9, 9), :]
        return 0

    lax.fori_loop(0, LON, body, 0)


def legendre_tables(q, start_ref, slope_ref, lag_ref, trig_ref, p_ref):
    wave = (lanes((1, 128)) % MDEV + q * MDEV).astype(F32)

    def coefficients(block, _):
        offsets = (lax.broadcasted_iota(jnp.int32, (64, 128), 0) + block * 64).astype(F32)
        degree = wave + offsets
        spacing = jnp.maximum(offsets * (2.0 * wave + offsets), 1.0)
        slope = jnp.sqrt(jnp.maximum(4.0 * degree * degree - 1.0, 0.0) / spacing)
        numerator = (2.0 * degree + 1.0) * (offsets - 1.0) * (degree - 1.0 + wave)
        lag = jnp.sqrt(jnp.maximum(numerator, 0.0) / (jnp.maximum(2.0 * degree - 3.0, 1.0) * spacing))
        first = offsets < 0.5
        slope_ref[block_rows(block, 64), :] = jnp.where(first, 0.0, slope)
        lag_ref[block_rows(block, 64), :] = jnp.where(first, 1.0, lag)
        return 0

    lax.fori_loop(0, WAVES // 64, coefficients, 0)
    row = lax.broadcasted_iota(jnp.int32, (ROWS, 128), 0)
    colat = (row % 16) * 24 + (row // 16) * 8 + lanes((ROWS, 128)) // MDEV
    theta = math.pi * (colat.astype(F32) + 0.5) / NLAT
    mu = jnp.cos(theta)
    sine = jnp.sin(theta)
    trig_ref[...] = sine * (WAVES * math.pi / NLAT)
    log_sine = jnp.log(sine) * (1.0 / math.log(2.0))
    coarse = jnp.floor(log_sine * 1024.0) * (1.0 / 1024.0)
    whole = wave * coarse
    exponent = jnp.floor(whole)
    fraction = (whole - exponent) + wave * (log_sine - coarse) + start_ref[pl.ds(q, 1), :]
    lower = -jnp.exp2(fraction)
    upper = jnp.zeros_like(lower)

    def body(block, carry):
        upper, lower, exponent = carry
        growth = jnp.exp2(jnp.maximum(exponent, -140.0))
        for offset in range(8):
            k = block * 8 + offset
            moved = (slope_ref[pl.ds(k, 1), :] * mu) * upper - lag_ref[pl.ds(k, 1), :] * lower
            upper, lower = moved, upper
            inside = wave + k.astype(F32) <= WAVES - 1.0
            p_ref[block_rows(k, ROWS), :] = jnp.where(inside, upper * growth, 0.0)
        big = jnp.maximum(jnp.abs(upper), jnp.abs(lower)) > 2.0**32
        scale = jnp.where(big, 2.0**-32, 1.0)
        return upper * scale, lower * scale, exponent + jnp.where(big, 32.0, 0.0)

    lax.fori_loop(0, WAVES // 8, body, (upper, lower, exponent))


def forward_operand(r_ref, x_ref):
    lane = lanes((16, 128))

    def body(pair, _):
        columns = [
            [r_ref[pl.ds((2 * pair + par) * MSG_G + c, 16, stride=3), :] for c in range(3)] for par in range(2)
        ]
        for a in range(GROUPS):
            first, offset = divmod(BLK * a, 128)
            pieces = []
            for par in range(2):
                source = columns[par][first]
                if offset + BLK > 128:
                    source = jnp.where(lane >= offset, source, columns[par][first + 1])
                shift = (64 * par - offset) % 128
                pieces.append(pltpu.roll(source, shift, 1) if shift else source)
            high, low = split(jnp.where(lane < 64, pieces[0], pieces[1]))
            x_ref[a * 16 : (a + 1) * 16, block_rows(pair, 128)] = high
            x_ref[128 + a * 16 : 128 + (a + 1) * 16, block_rows(pair, 128)] = low
        return 0

    lax.fori_loop(0, LON // 2, body, 0)


def product(x_ref, high_ref, low_ref, block):
    columns = block_rows(block, 256)
    both = jnp.dot(x_ref[...], high_ref[:, columns], preferred_element_type=F32)
    rest = jnp.dot(x_ref[0:128, :], low_ref[:, columns], preferred_element_type=F32)
    return both[0:128] + both[128:256] + rest


def forward_transform(q, south, x_ref, high_ref, low_ref, block_ref, m_ref, send):
    def body(step, _):
        block = (step + q // 8) % 4
        block_ref[...] = product(x_ref, high_ref, low_ref, block)
        for half in range(2):
            items = swap_groups(
                [block_ref[block_rows(mirrored(south, a), 16), half * 128 : (half + 1) * 128] for a in range(GROUPS)]
            )
            for group in range(GROUPS):
                owner = block * 8 + half * 4 + group // 2
                m_ref[pl.ds(owner * MSG_C + (group % 2) * 9, 9), :] = items[group][0:9]
            for index in range(4):
                send(block * 8 + half * 4 + index)
        return 0

    lax.fori_loop(0, 4, body, 0)


def analysis(g_ref, trig_ref, even_ref, odd_ref, p_ref, a_ref):
    for f in range(3):
        for r in range(2):
            for s in range(3):
                north = g_ref[pl.ds(r * 9 + f * 3 + s, 16, stride=MSG_C), :]
                south = g_ref[pl.ds(16 * MSG_C + r * 9 + f * 3 + 2 - s, 16, stride=MSG_C), :]
                weight = trig_ref[s * 16 : (s + 1) * 16, :]
                rows = slice((f * 2 + r) * ROWS + s * 16, (f * 2 + r) * ROWS + (s + 1) * 16)
                even_ref[rows, :] = (north + south) * weight
                odd_ref[rows, :] = (north - south) * weight

    def body(block, _):
        totals = [[None] * 8 for _ in range(FR)]
        for parity, source in ((0, even_ref), (1, odd_ref)):
            planes = [p_ref[block_rows(block * 8 + k, ROWS), :] for k in range(parity, 8, 2)]
            for fr in range(FR):
                field = source[fr * ROWS : (fr + 1) * ROWS, :]
                for index, plane in enumerate(planes):
                    terms = plane * field
                    pieces = [terms[8 * n : 8 * n + 8] for n in range(6)]
                    total = (pieces[0] + pieces[1]) + (pieces[2] + pieces[3]) + (pieces[4] + pieces[5])
                    totals[fr][parity + 2 * index] = total
        for fr in range(FR):
            a_ref[pl.ds(pl.multiple_of(fr * WAVES + block * 8, 8), 8), :] = fold_rows(totals[fr])
        return 0

    lax.fori_loop(0, WAVES // 8, body, 0)


def update(q, stiff, damp, state_ref, a_ref, ns_ref, st_ref):
    wave = (lax.broadcasted_iota(jnp.int32, (MDEV, WAVES), 0) + q * MDEV).astype(F32)
    degree = wave + lanes((MDEV, WAVES)).astype(F32)
    ratio = degree * (degree + 1.0) / (WAVES * (WAVES - 1.0))
    inside = degree <= WAVES - 1.0
    denominator = 1.0 + stiff * ratio
    damped = jnp.where(inside, 1.0 / (1.0 + damp * ratio * ratio), 0.0)

    def total(fr):
        turned = jnp.transpose(a_ref[fr * WAVES : (fr + 1) * WAVES, :])
        pieces = [turned[16 * n : 16 * n + 16] for n in range(GROUPS)]
        summed = ((pieces[0] + pieces[1]) + (pieces[2] + pieces[3])) + ((pieces[4] + pieces[5]) + (pieces[6] + pieces[7]))
        return state_ref[fr * MDEV : (fr + 1) * MDEV, :] + summed

    def put(fr, value):
        ns_ref[fr * MDEV : (fr + 1) * MDEV, :] = value
        st_ref[fr * WAVES : (fr + 1) * WAVES, :] = jnp.transpose(jnp.concatenate([value] * GROUPS, axis=0))

    for r in range(2):
        vorticity, divergence, height = total(r), total(2 + r), total(4 + r)
        put(r, vorticity * damped)
        put(2 + r, (divergence + ratio * height) / denominator * damped)
        put(4 + r, (height - stiff * divergence) / denominator * damped)


def synthesis(p_ref, st_ref, h_ref):
    for chunk in range(2):
        members = range(chunk * 3, chunk * 3 + 3)

        def body(block, carry):
            sums = list(carry)
            for k in range(8):
                plane = p_ref[block_rows(block * 8 + k, ROWS), :]
                for n, fr in enumerate(members):
                    value = st_ref[pl.ds(fr * WAVES + block * 8 + k, 1), :]
                    sums[2 * n + k % 2] = sums[2 * n + k % 2] + plane * value
            return tuple(sums)

        zero = jnp.zeros((ROWS, 128), F32)
        sums = lax.fori_loop(0, WAVES // 8, body, (zero,) * 6)
        for n, fr in enumerate(members):
            f, r = divmod(fr, 2)
            north = sums[2 * n] + sums[2 * n + 1]
            south = sums[2 * n] - sums[2 * n + 1]
            for s in range(3):
                rows = slice(s * 16, (s + 1) * 16)
                h_ref[pl.ds(r * 9 + f * 3 + s, 16, stride=MSG_C), :] = north[rows]
                h_ref[pl.ds(16 * MSG_C + r * 9 + f * 3 + 2 - s, 16, stride=MSG_C), :] = south[rows]


def inverse_operand(south, cp_ref, y_ref):
    def body(column, _):
        items = swap_groups(
            [cp_ref[pl.ds((column * 4 + g // 2) * MSG_C + (g % 2) * 9, 16), :] for g in range(GROUPS)]
        )
        for a in range(GROUPS):
            row = mirrored(south, a)
            high, low = split(items[a])
            y_ref[block_rows(row, 16), block_rows(column, 128)] = high
            y_ref[block_rows(row + GROUPS, 16), block_rows(column, 128)] = low
        return 0

    lax.fori_loop(0, 2 * WAVES // 128, body, 0)


def inverse_transform(q, y_ref, high_ref, low_ref, block_ref, w_ref, send):
    lane = lanes((16, 128))

    def body(step, _):
        block = (step + q // 4) % 8
        block_ref[...] = product(y_ref, high_ref, low_ref, block)
        for index in range(4):
            half, par = divmod(index, 2)
            owner = block * 4 + index
            columns = [None] * 3
            for a in range(GROUPS):
                first, offset = divmod(BLK * a, 128)
                piece = block_ref[a * 16 : (a + 1) * 16, half * 128 : (half + 1) * 128]
                shift = (offset - 64 * par) % 128
                piece = pltpu.roll(piece, shift, 1) if shift else piece
                if columns[first] is None:
                    columns[first] = piece
                else:
                    columns[first] = jnp.where(lane >= offset, piece, columns[first])
                if offset + BLK > 128:
                    columns[first + 1] = piece
            for c in range(3):
                w_ref[pl.ds(owner * MSG_G + c, 9, stride=3), :] = columns[c][0:9]
            send(owner)
        return 0

    lax.fori_loop(0, 8, body, 0)


def scatter_rows(o_ref, out_ref):
    def body(d, _):
        c, h = d // 2, d % 2
        for f in range(3):
            out_ref[pl.ds((f * MODES + c) * 18 + h * 9, 9), :] = o_ref[pl.ds(d * MSG_G + f * 9, 9), :]
        return 0

    lax.fori_loop(0, LON, body, 0)


def slot_of(source):
    return jnp.where(source < 16, source, 47 - source)


def kernel(
    t_ref,
    state_ref,
    start_ref,
    stiff_ref,
    damp_ref,
    fh_any,
    fl_any,
    ih_any,
    il_any,
    ns_ref,
    out_ref,
    fh_ref,
    fl_ref,
    ih_ref,
    il_ref,
    sb_ref,
    r_ref,
    x_ref,
    fblock_ref,
    m_ref,
    g_ref,
    even_ref,
    odd_ref,
    slope_ref,
    lag_ref,
    trig_ref,
    p_ref,
    a_ref,
    st_ref,
    h_ref,
    cp_ref,
    y_ref,
    iblock_ref,
    w_ref,
    o_ref,
    const_sem,
    send_sem,
    recv_sem,
):
    q = lax.axis_index("lon")
    p = lax.axis_index("lat")
    owned = q // 2
    half = q % 2
    south = p >= LAT // 2
    my_source = slot_of(p * 2 + half)

    loads = [
        pltpu.make_async_copy(source, target, const_sem.at[index])
        for index, (source, target) in enumerate(
            ((fh_any, fh_ref), (fl_any, fl_ref), (ih_any, ih_ref), (il_any, il_ref))
        )
    ]
    for load in loads:
        load.start()

    def grid_peer(n):
        return n, p

    def wave_peer(n):
        return n, owned

    def row_peer(n):
        source = slot_of(n)
        return p * 2 + source % 2, source // 2

    def message(stage, n):
        if stage == 0:
            return grid_peer(n), sb_ref.at[pl.ds(n * MSG_G, MSG_G)], r_ref, q, MSG_G
        if stage == 1:
            return wave_peer(n), m_ref.at[pl.ds(n * MSG_C, MSG_C)], g_ref, my_source, MSG_C
        if stage == 2:
            return row_peer(n), h_ref.at[pl.ds(n * MSG_C, MSG_C)], cp_ref, q, MSG_C
        return grid_peer(n), w_ref.at[pl.ds(n * MSG_G, MSG_G)], o_ref, q, MSG_G

    def remote(stage, n):
        (lon, lat), source, target, slot, size = message(stage, n)
        here = jnp.logical_and(lon == q, lat == p)
        copy = pltpu.make_async_remote_copy(
            src_ref=source,
            dst_ref=target.at[pl.ds(slot * size, size)],
            send_sem=send_sem.at[stage, n],
            recv_sem=recv_sem.at[stage, slot],
            device_id=(lon, lat),
            device_id_type=MESH,
        )
        return here, copy

    def send(stage, n):
        (lon, lat), source, target, slot, size = message(stage, n)
        here, copy = remote(stage, n)

        @pl.when(jnp.logical_not(here))
        def _():
            copy.start()

        @pl.when(here)
        def _():
            pltpu.make_async_copy(
                source, target.at[pl.ds(slot * size, size)], recv_sem.at[stage, slot]
            ).start()

    def finish(stage):
        def body(n, _):
            here, copy = remote(stage, n)

            @pl.when(jnp.logical_not(here))
            def _():
                copy.wait_send()

            return 0

        lax.fori_loop(0, 32, body, 0)

    def receive(stage):
        size = MSG_G if stage in (0, 3) else MSG_C
        target = (r_ref, g_ref, cp_ref, o_ref)[stage]

        def body(n, _):
            part = target.at[pl.ds(n * size, size)]
            pltpu.make_async_copy(part, part, recv_sem.at[stage, n]).wait()
            return 0

        lax.fori_loop(0, 32, body, 0)

    barrier = pltpu.get_barrier_semaphore()

    def greet(n, _):
        for peer in (grid_peer, wave_peer, row_peer):
            lon, lat = peer(n)

            @pl.when(jnp.logical_not(jnp.logical_and(lon == q, lat == p)))
            def _():
                pl.semaphore_signal(barrier, inc=1, device_id=(lon, lat), device_id_type=MESH)

        return 0

    lax.fori_loop(0, 32, greet, 0)
    gather_rows(t_ref, sb_ref)
    pl.semaphore_wait(barrier, jnp.where(owned == p, 93, 95))

    lax.fori_loop(0, LON, lambda n, _: (send(0, (n + q + 1) % LON), 0)[1], 0)
    legendre_tables(q, start_ref, slope_ref, lag_ref, trig_ref, p_ref)
    receive(0)
    forward_operand(r_ref, x_ref)
    loads[0].wait()
    loads[1].wait()
    forward_transform(q, south, x_ref, fh_ref, fl_ref, fblock_ref, m_ref, functools.partial(send, 1))
    receive(1)
    analysis(g_ref, trig_ref, even_ref, odd_ref, p_ref, a_ref)
    update(q, stiff_ref[p], damp_ref[p], state_ref, a_ref, ns_ref, st_ref)
    synthesis(p_ref, st_ref, h_ref)
    lax.fori_loop(0, 32, lambda n, _: (send(2, (n + q) % 32), 0)[1], 0)
    loads[2].wait()
    loads[3].wait()
    receive(2)
    inverse_operand(south, cp_ref, y_ref)
    inverse_transform(q, y_ref, ih_ref, il_ref, iblock_ref, w_ref, functools.partial(send, 3))
    receive(3)
    scatter_rows(o_ref, out_ref)
    for stage in range(4):
        finish(stage)


def body(tendency, state, stiffness, damping):
    fields, modes = tendency.shape[0], tendency.shape[1]
    rows = fields * modes * 18
    vmem = pl.BlockSpec(memory_space=pltpu.VMEM)
    smem = pl.BlockSpec(memory_space=pltpu.SMEM)
    anywhere = pl.BlockSpec(memory_space=pl.ANY)
    constants = fourier_constants()
    new_state, new_fields = pl.pallas_call(
        kernel,
        out_shape=(
            jax.ShapeDtypeStruct((FR * MDEV, WAVES), F32),
            jax.ShapeDtypeStruct((rows, 128), F32),
        ),
        in_specs=[vmem, vmem, vmem, smem, smem] + [anywhere] * 4,
        out_specs=(vmem, vmem),
        scratch_shapes=[
            pltpu.VMEM((64 * LON, 2 * WAVES), BF16),
            pltpu.VMEM((64 * LON, 2 * WAVES), BF16),
            pltpu.VMEM((2 * WAVES, 64 * LON), BF16),
            pltpu.VMEM((2 * WAVES, 64 * LON), BF16),
            pltpu.VMEM((LON * MSG_G, 128), F32),
            pltpu.VMEM((LON * MSG_G + 32, 128), F32),
            pltpu.VMEM((256, 64 * LON), BF16),
            pltpu.VMEM((128, 256), F32),
            pltpu.VMEM((32 * MSG_C, 128), F32),
            pltpu.VMEM((32 * MSG_C, 128), F32),
            pltpu.VMEM((FR * ROWS, 128), F32),
            pltpu.VMEM((FR * ROWS, 128), F32),
            pltpu.VMEM((WAVES, 128), F32),
            pltpu.VMEM((WAVES, 128), F32),
            pltpu.VMEM((ROWS, 128), F32),
            pltpu.VMEM((WAVES * ROWS, 128), F32),
            pltpu.VMEM((FR * WAVES, 128), F32),
            pltpu.VMEM((FR * WAVES, 128), F32),
            pltpu.VMEM((32 * MSG_C, 128), F32),
            pltpu.VMEM((32 * MSG_C + 16, 128), F32),
            pltpu.VMEM((256, 2 * WAVES), BF16),
            pltpu.VMEM((128, 256), F32),
            pltpu.VMEM((LON * MSG_G, 128), F32),
            pltpu.VMEM((LON * MSG_G, 128), F32),
            pltpu.SemaphoreType.DMA((4,)),
            pltpu.SemaphoreType.DMA((4, 32)),
            pltpu.SemaphoreType.DMA((4, 32)),
        ],
        compiler_params=pltpu.CompilerParams(
            collective_id=0, has_side_effects=True, vmem_limit_bytes=52 * 2**20
        ),
        name="spectral_step",
    )(
        tendency.reshape(rows, 128),
        state.reshape(FR * MDEV, WAVES),
        jnp.asarray(start_constants()),
        stiffness,
        damping,
        *[jnp.asarray(table) for table in constants],
    )
    return new_state.reshape(state.shape), new_fields.reshape(tendency.shape)


def solution(mesh):
    return jax.shard_map(
        body,
        mesh=mesh,
        in_specs=(P(None, None, "lat", "lon", None), P("lat", None, None, "lon", None), P(), P()),
        out_specs=(P("lat", None, None, "lon", None), P(None, None, "lat", "lon", None)),
        check_vma=False,
    )
```

profile of v0, /device:TPU:1, one launch (start us, length us, event | category | flops | bytes accessed | tf_op | source)
XLA Modules:
  0.0 112.3 jit_solution(3359485341550304075)
XLA Ops:
  0.6 0.0 copy-start
  0.6 1.0 copy-done
  1.6 0.0 copy-start.1
  1.6 0.9 copy-done.1
  2.6 0.0 copy-start.2
  2.6 0.7 copy-done.2
  3.3 0.0 copy-start.3
  3.3 0.7 copy-done.3
  3.9 0.0 copy-start.4
  3.9 0.7 copy-done.4
  4.6 106.2 %spectral_step.1 = (f32[96,512]{1,0:T(8,128)S(1)}, f32[864,128]{1,0:T(8,128)S(1)}) custom-call(f32[864,128]{1,0:T(8,128)S(1)} %bitcast.5, f32[96,512]{1,0:T(8,128)S(1)} %bitcast.6, f32[32,128]{1,0:T(8,128)S(1)} %copy-done.2, f32[16]{0:T(128)S(1)} %copy-done.3, f32[16]{0:T(128)S(1)} %copy-done.4, bf16[2048,1024]{1,0:T(8,128)(2,1)} %constant.11.clone.fh_any, ...), custom_call_target="tpu_custom_call" | custom-call | tf_op jit(solution)/shard_map/spectral_step/pallas_call | solution.py:528
  110.9 0.7 copy.14
  111.5 0.8 copy.15
Async XLA Ops:
  0.6 1.0 copy-start
  1.6 0.9 copy-start.1
  2.6 0.7 copy-start.2
  3.3 0.7 copy-start.3
  3.9 0.7 copy-start.4
where the time goes:
time: 114 us; the launch traced here: 112 us
  Pallas kernels  106 us (93%)
  local copies, waits for them, and re-layouts  5.4 us (5%)
    pallas_call x1, Pallas kernels, body(): pl.pallas_call(kernel, out_shape=(jax.ShapeDtypeStruct((FR * MDEV, WAVES)...  106 us
    unnamed x12, local copies, waits for them, and re-layouts  5.4 us

commit v1 on v0

v1 whole, which is shorter than its diff:
```python
import functools
import math

import jax
import jax.numpy as jnp
import ml_dtypes
import numpy as np
from jax import lax
from jax.experimental import pallas as pl
from jax.experimental.pallas import tpu as pltpu
from jax.sharding import PartitionSpec as P

NLAT = 768
NLON = 1536
WAVES = 512
MODES = 16
LON = 32
LAT = 16
BLK = 48
MDEV = 16
GROUPS = 8
MSG_G = 27
SLOT_G = 48
SLOT_C = 32
MSG_C = 18
FR = 6
PLANE = 384
ROWS = 48
MESH = pl.DeviceIdType.MESH
F32 = jnp.float32
BF16 = jnp.bfloat16


def split_constant(table):
    high = table.astype(np.float32).astype(ml_dtypes.bfloat16)
    low = (table - high.astype(np.float64)).astype(np.float32).astype(ml_dtypes.bfloat16)
    return high, low


def lon_of(place):
    return (place % 8) * 4 + place // 8


def place_of(lon):
    return (lon % 4) * 8 + lon // 4


@functools.lru_cache(maxsize=None)
def fourier_constants():
    slot = np.arange(LON * 64)
    block, inner = lon_of(slot // 64), slot % 64
    lon = block * BLK + inner
    valid = (inner < BLK)[:, None]
    wave = np.arange(WAVES)
    angle = 2.0 * np.pi / NLON * ((lon[:, None] * wave[None, :]) % NLON)
    owners = lon_of(np.arange(LON))
    cosine = np.where(valid, np.cos(angle), 0.0).reshape(-1, LON, MDEV)[:, owners]
    sine = np.where(valid, np.sin(angle), 0.0).reshape(-1, LON, MDEV)[:, owners]
    basis = np.stack([cosine, -sine], axis=2).reshape(LON * 64, 2 * WAVES)
    factor = np.where(wave == 0, 1.0, 2.0).reshape(LON, 1, MDEV) / WAVES
    factor = np.broadcast_to(factor[owners], (LON, 2, MDEV)).reshape(2 * WAVES, 1)
    return split_constant(basis / NLON) + split_constant(factor * basis.T)


@functools.lru_cache(maxsize=None)
def start_constants():
    start = [
        (0.5 * math.log(m + 0.5) + 0.5 * math.lgamma(m + 0.5) - 0.5 * math.lgamma(m + 1.0) - 0.25 * math.log(math.pi))
        / math.log(2.0)
        for m in range(WAVES)
    ]
    return np.tile(np.array(start, np.float32).reshape(LON, MDEV), (1, GROUPS))


def lanes(shape):
    return lax.broadcasted_iota(jnp.int32, shape, len(shape) - 1)


def swap_groups(items):
    group = lanes(items[0].shape) // 16
    items = list(items)
    for step in (4, 2, 1):
        keep = (group & step) == 0
        for low in range(GROUPS):
            if low & step:
                continue
            high = low + step
            x, y = items[low], items[high]
            items[low] = jnp.where(keep, x, pltpu.roll(y, 16 * step, 1))
            items[high] = jnp.where(keep, pltpu.roll(x, 128 - 16 * step, 1), y)
    return items


def fold_rows(parts):
    row = lax.broadcasted_iota(jnp.int32, (8, 128), 0)
    upper = row < 4
    four = []
    for index in range(4):
        x, y = parts[index], parts[index + 4]
        four.append(jnp.where(upper, x, y) + pltpu.roll(jnp.where(upper, y, x), 4, 0))
    for step in (2, 1):
        keep = (row & step) == 0
        four = [
            jnp.where(
                keep,
                four[index] + pltpu.roll(four[index], 8 - step, 0),
                four[index + step] + pltpu.roll(four[index + step], step, 0),
            )
            for index in range(step)
        ]
    return four[0]


def split(x):
    high = x.astype(BF16)
    return high, (x - high.astype(F32)).astype(BF16)


def mirrored(south, a):
    return jnp.where(south, GROUPS - 1 - a, a)


def block_rows(index, size):
    return pl.ds(pl.multiple_of(index * size, size), size)


def gather_rows(t_ref, sb_ref):
    def body(d, _):
        c, h = d // 2, d % 2
        for f in range(3):
            sb_ref[pl.ds(d * MSG_G + f * 9, 9), :] = t_ref[pl.ds((f * MODES + c) * 18 + h * 9, 9), :]
        return 0

    lax.fori_loop(0, LON, body, 0)


def legendre_tables(q, start_ref, slope_ref, lag_ref, trig_ref, p_ref):
    wave = (lanes((1, 128)) % MDEV + q * MDEV).astype(F32)

    def coefficients(block, _):
        offsets = (lax.broadcasted_iota(jnp.int32, (64, 128), 0) + block * 64).astype(F32)
        degree = wave + offsets
        spacing = jnp.maximum(offsets * (2.0 * wave + offsets), 1.0)
        slope = jnp.sqrt(jnp.maximum(4.0 * degree * degree - 1.0, 0.0) / spacing)
        numerator = (2.0 * degree + 1.0) * (offsets - 1.0) * (degree - 1.0 + wave)
        lag = jnp.sqrt(jnp.maximum(numerator, 0.0) / (jnp.maximum(2.0 * degree - 3.0, 1.0) * spacing))
        first = offsets < 0.5
        slope_ref[block_rows(block, 64), :] = jnp.where(first, 0.0, slope)
        lag_ref[block_rows(block, 64), :] = jnp.where(first, 1.0, lag)
        return 0

    lax.fori_loop(0, WAVES // 64, coefficients, 0)
    row = lax.broadcasted_iota(jnp.int32, (ROWS, 128), 0)
    colat = ((row // 24) * 8 + row % 8) * 24 + (row // 8 % 3) * 8 + lanes((ROWS, 128)) // MDEV
    theta = math.pi * (colat.astype(F32) + 0.5) / NLAT
    mu = jnp.cos(theta)
    sine = jnp.sin(theta)
    trig_ref[...] = sine * (WAVES * math.pi / NLAT)
    log_sine = jnp.log(sine) * (1.0 / math.log(2.0))
    coarse = jnp.floor(log_sine * 1024.0) * (1.0 / 1024.0)
    whole = wave * coarse
    exponent = jnp.floor(whole)
    fraction = (whole - exponent) + wave * (log_sine - coarse) + start_ref[pl.ds(q, 1), :]
    lower = -jnp.exp2(fraction)
    upper = jnp.zeros_like(lower)

    def body(block, carry):
        upper, lower, exponent = carry
        growth = jnp.exp2(jnp.maximum(exponent, -140.0))
        for offset in range(8):
            k = block * 8 + offset
            moved = (slope_ref[pl.ds(k, 1), :] * mu) * upper - lag_ref[pl.ds(k, 1), :] * lower
            upper, lower = moved, upper
            inside = wave + k.astype(F32) <= WAVES - 1.0
            p_ref[pl.ds(block * PLANE + offset, ROWS, stride=8), :] = jnp.where(inside, upper * growth, 0.0)
        big = jnp.maximum(jnp.abs(upper), jnp.abs(lower)) > 2.0**32
        scale = jnp.where(big, 2.0**-32, 1.0)
        return upper * scale, lower * scale, exponent + jnp.where(big, 32.0, 0.0)

    lax.fori_loop(0, WAVES // 8, body, (upper, lower, exponent))


def forward_operand(group, r_ref, x_ref):
    lane = lanes((16, 128))

    def body(pair, _):
        first_row = (group * 8 + 2 * pair) * SLOT_G
        columns = [[r_ref[pl.ds(first_row + par * SLOT_G + c, 16, stride=3), :] for c in range(3)] for par in range(2)]
        for a in range(GROUPS):
            first, offset = divmod(BLK * a, 128)
            pieces = []
            for par in range(2):
                source = columns[par][first]
                if offset + BLK > 128:
                    source = jnp.where(lane >= offset, source, columns[par][first + 1])
                shift = (64 * par - offset) % 128
                pieces.append(pltpu.roll(source, shift, 1) if shift else source)
            high, low = split(jnp.where(lane < 64, pieces[0], pieces[1]))
            x_ref[a * 16 : (a + 1) * 16, block_rows(pair, 128)] = high
            x_ref[128 + a * 16 : 128 + (a + 1) * 16, block_rows(pair, 128)] = low
        return 0

    lax.fori_loop(0, 4, body, 0)


def product(x_ref, high_ref, low_ref, rows, columns):
    both = jnp.dot(x_ref[...], high_ref[rows, columns], preferred_element_type=F32)
    rest = jnp.dot(x_ref[0:128, :], low_ref[rows, columns], preferred_element_type=F32)
    return both[0:128] + both[128:256] + rest


def add_products(group, x_ref, high_ref, low_ref, sum_ref):
    rows = block_rows(group, x_ref.shape[1])

    def body(block, _):
        columns = block_rows(block, 256)
        sum_ref[:, columns] += product(x_ref, high_ref, low_ref, rows, columns)
        return 0

    lax.fori_loop(0, sum_ref.shape[1] // 256, body, 0)


def forward_blocks(q, south, group, x_ref, high_ref, low_ref, sum_ref, block_ref, m_ref, send):
    rows = block_rows(group, x_ref.shape[1])

    def body(step, _):
        block = (step + q % 4) % 4
        columns = block_rows(block, 256)
        block_ref[...] = sum_ref[:, columns] + product(x_ref, high_ref, low_ref, rows, columns)
        for half in range(2):
            items = swap_groups(
                [block_ref[block_rows(mirrored(south, a), 16), half * 128 : (half + 1) * 128] for a in range(GROUPS)]
            )
            for group in range(GROUPS):
                owner = block * 8 + half * 4 + group // 2
                m_ref[pl.ds(owner * MSG_C + (group % 2) * 9, 9), :] = items[group][0:9]
            for index in range(4):
                send(block * 8 + half * 4 + index)
        return 0

    lax.fori_loop(0, 4, body, 0)


def analysis(g_ref, trig_ref, eo_ref, p_ref, a_ref):
    for n in range(2):
        for s in range(3):
            weight = trig_ref[n * 24 + s * 8 : n * 24 + s * 8 + 8, :]
            for f in range(3):
                for r in range(2):
                    north = g_ref[pl.ds(n * 8 * MSG_C + r * 9 + f * 3 + s, 8, stride=MSG_C), :]
                    south = g_ref[pl.ds((16 + n * 8) * MSG_C + r * 9 + f * 3 + 2 - s, 8, stride=MSG_C), :]
                    first = (f * 2 + r) * PLANE + (n * 24 + s * 8) * 8
                    even, odd = (north + south) * weight, (north - south) * weight
                    for k in range(8):
                        eo_ref[pl.ds(first + k, 8, stride=8), :] = odd if k % 2 else even

    def body(quad, _):
        def rows(group, sums):
            sums = list(sums)
            for row in range(8):
                first = (group * 8 + row) * 8
                fields = [eo_ref[pl.ds(pl.multiple_of(fr * PLANE + first, 8), 8), :] for fr in range(FR)]
                for b in range(4):
                    plane = p_ref[pl.ds(pl.multiple_of((quad * 4 + b) * PLANE + first, 8), 8), :]
                    for fr in range(FR):
                        sums[b * FR + fr] = sums[b * FR + fr] + plane * fields[fr]
            return tuple(sums)

        sums = lax.fori_loop(0, ROWS // 8, rows, (jnp.zeros((8, 128), F32),) * (4 * FR))
        for b in range(4):
            for fr in range(FR):
                a_ref[pl.ds(pl.multiple_of(fr * WAVES + (quad * 4 + b) * 8, 8), 8), :] = sums[b * FR + fr]
        return 0

    lax.fori_loop(0, WAVES // 32, body, 0)


def update(q, stiff, damp, state_ref, a_ref, ns_ref, st_ref):
    wave = (lax.broadcasted_iota(jnp.int32, (MDEV, WAVES), 0) + q * MDEV).astype(F32)
    degree = wave + lanes((MDEV, WAVES)).astype(F32)
    ratio = degree * (degree + 1.0) / (WAVES * (WAVES - 1.0))
    inside = degree <= WAVES - 1.0
    denominator = 1.0 + stiff * ratio
    damped = jnp.where(inside, 1.0 / (1.0 + damp * ratio * ratio), 0.0)

    def total(fr):
        turned = jnp.transpose(a_ref[fr * WAVES : (fr + 1) * WAVES, :])
        pieces = [turned[16 * n : 16 * n + 16] for n in range(GROUPS)]
        summed = ((pieces[0] + pieces[1]) + (pieces[2] + pieces[3])) + ((pieces[4] + pieces[5]) + (pieces[6] + pieces[7]))
        return state_ref[fr * MDEV : (fr + 1) * MDEV, :] + summed

    def put(fr, value):
        ns_ref[fr * MDEV : (fr + 1) * MDEV, :] = value
        st_ref[fr * WAVES : (fr + 1) * WAVES, :] = jnp.transpose(jnp.concatenate([value] * GROUPS, axis=0))

    for r in range(2):
        vorticity, divergence, height = total(r), total(2 + r), total(4 + r)
        put(r, vorticity * damped)
        put(2 + r, (divergence + ratio * height) / denominator * damped)
        put(4 + r, (height - stiff * divergence) / denominator * damped)


def synthesis(p_ref, st_ref, h_ref):
    sign = jnp.where(lax.broadcasted_iota(jnp.int32, (8, 128), 0) % 2 == 0, 1.0, -1.0)

    def body(group, _):
        n, s = group // 3, group % 3
        for chunk in range(2):

            def degrees(block, sums):
                sums = list(sums)
                for b in range(2):
                    first = (block * 2 + b) * PLANE + group * 64
                    values = [
                        st_ref[pl.ds(pl.multiple_of((chunk * 3 + m) * WAVES + (block * 2 + b) * 8, 8), 8), :]
                        for m in range(3)
                    ]
                    for row in range(8):
                        plane = p_ref[pl.ds(pl.multiple_of(first + row * 8, 8), 8), :]
                        for m in range(3):
                            sums[m * 8 + row] = sums[m * 8 + row] + plane * values[m]
                return tuple(sums)

            sums = lax.fori_loop(0, WAVES // 16, degrees, (jnp.zeros((8, 128), F32),) * 24)
            for m in range(3):
                f, r = divmod(chunk * 3 + m, 2)
                parts = list(sums[m * 8 : m * 8 + 8])
                line = r * 9 + f * 3
                h_ref[pl.ds(n * 8 * MSG_C + line + s, 8, stride=MSG_C), :] = fold_rows(parts)
                parts = [part * sign for part in parts]
                h_ref[pl.ds((16 + n * 8) * MSG_C + line + 2 - s, 8, stride=MSG_C), :] = fold_rows(parts)
        return 0

    lax.fori_loop(0, ROWS // 8, body, 0)


def inverse_operand(group, south, cp_ref, y_ref):
    for column in range(2):
        first = (group * 8 + column * 4) * SLOT_C
        items = swap_groups([cp_ref[pl.ds(first + g // 2 * SLOT_C + g % 2 * 9, 16), :] for g in range(GROUPS)])
        for a in range(GROUPS):
            row = mirrored(south, a)
            high, low = split(items[a])
            y_ref[block_rows(row, 16), column * 128 : (column + 1) * 128] = high
            y_ref[block_rows(row + GROUPS, 16), column * 128 : (column + 1) * 128] = low


def inverse_blocks(q, group, y_ref, high_ref, low_ref, sum_ref, block_ref, w_ref, send):
    lane = lanes((16, 128))
    rows = block_rows(group, y_ref.shape[1])

    def body(step, _):
        block = (step + q % 4 * 2) % 8
        columns = block_rows(block, 256)
        block_ref[...] = sum_ref[:, columns] + product(y_ref, high_ref, low_ref, rows, columns)
        for index in range(4):
            half, par = divmod(index, 2)
            owner = block * 4 + index
            columns = [None] * 3
            for a in range(GROUPS):
                first, offset = divmod(BLK * a, 128)
                piece = block_ref[a * 16 : (a + 1) * 16, half * 128 : (half + 1) * 128]
                shift = (offset - 64 * par) % 128
                piece = pltpu.roll(piece, shift, 1) if shift else piece
                if columns[first] is None:
                    columns[first] = piece
                else:
                    columns[first] = jnp.where(lane >= offset, piece, columns[first])
                if offset + BLK > 128:
                    columns[first + 1] = piece
            for c in range(3):
                w_ref[pl.ds(owner * MSG_G + c, 9, stride=3), :] = columns[c][0:9]
            send(owner)
        return 0

    lax.fori_loop(0, 8, body, 0)


def slot_of(source):
    return jnp.where(source < 16, source, 47 - source)


def kernel(
    t_any,
    state_any,
    start_any,
    stiff_any,
    damp_any,
    fh_any,
    fl_any,
    ih_any,
    il_any,
    ns_ref,
    o_ref,
    t_ref,
    state_ref,
    start_ref,
    stiff_ref,
    damp_ref,
    fh_ref,
    fl_ref,
    ih_ref,
    il_ref,
    sb_ref,
    r_ref,
    x_ref,
    fsum_ref,
    block_ref,
    m_ref,
    g_ref,
    eo_ref,
    slope_ref,
    lag_ref,
    trig_ref,
    p_ref,
    a_ref,
    st_ref,
    h_ref,
    cp_ref,
    y_ref,
    isum_ref,
    w_ref,
    load_sem,
    send_sem,
    recv_sem,
    ready_sem,
):
    q = lax.axis_index("lon")
    p = lax.axis_index("lat")
    here = place_of(q)
    south = p >= LAT // 2
    owned, half = q // 2, q % 2
    my_source = slot_of(p * 2 + half)
    back_mode = (q // 4 + 16 - p // 2 - p % 2 * 4) % 8 * 2 + q % 4 // 2
    back_half = q % 2
    back_slot = slot_of(p * 2 + back_half)

    barrier = pltpu.get_barrier_semaphore()

    def greet_lon(n, _):
        pl.semaphore_signal(barrier, inc=1, device_id=((q + n) % LON, p), device_id_type=MESH)
        return 0

    def greet_lat(n, _):
        pl.semaphore_signal(barrier, inc=1, device_id=(q, (p + n) % LAT), device_id_type=MESH)
        return 0

    lax.fori_loop(1, LON, greet_lon, 0)
    lax.fori_loop(1, LAT, greet_lat, 0)

    loads = [
        pltpu.make_async_copy(source, target, load_sem.at[index])
        for index, (source, target) in enumerate(
            (
                (t_any, t_ref),
                (start_any, start_ref),
                (fh_any, fh_ref),
                (fl_any, fl_ref),
                (state_any, state_ref),
                (stiff_any, stiff_ref),
                (damp_any, damp_ref),
                (ih_any, ih_ref),
                (il_any, il_ref),
            )
        )
    ]
    for load in loads:
        load.start()

    def copy(source, target, stage, group, peer):
        return pltpu.make_async_remote_copy(
            src_ref=source,
            dst_ref=target,
            send_sem=send_sem.at[stage],
            recv_sem=recv_sem.at[stage, group],
            device_id=peer,
            device_id_type=MESH,
        )

    def copy_or_keep(source, target, stage, group, peer):
        lon, lat = peer
        own = jnp.logical_and(lon == q, lat == p)

        @pl.when(jnp.logical_not(own))
        def _():
            copy(source, target, stage, group, peer).start()

        @pl.when(own)
        def _():
            pltpu.make_async_copy(source, target, recv_sem.at[stage, group]).start()

    def wait(ref, first, rows, sem):
        part = ref.at[pl.ds(first, rows)]
        pltpu.make_async_copy(part, part, sem).wait()

    def send_grid(n, _):
        place = (here // 8 + n // 8) % 4 * 8 + (here + n) % 8
        lon = lon_of(place)
        copy(sb_ref.at[pl.ds(lon * MSG_G, MSG_G)], r_ref.at[pl.ds(here * SLOT_G, MSG_G)], 0, here // 8, (lon, p)).start()
        return 0

    def send_waves(place):
        copy_or_keep(
            m_ref.at[pl.ds(place * MSG_C, MSG_C)],
            g_ref.at[pl.ds(my_source * MSG_C, MSG_C)],
            1,
            0,
            (lon_of(place), owned),
        )

    def send_rows(n, _):
        slot = (here // 8 + n // 8) % 4 * 8 + (here + n) % 8
        source = slot_of(slot)
        lat = source // 2
        lon = (p // 2 + lat // 2 + lat % 2 * 4) % 8 * 4 + p % 2 * 2 + source % 2
        copy_or_keep(
            h_ref.at[pl.ds(slot * MSG_C, MSG_C)],
            cp_ref.at[pl.ds(here * SLOT_C, MSG_C)],
            2,
            here // 8,
            (lon, lat),
        )
        return 0

    back_rows = pl.ds((back_mode * 2 + back_half) * MSG_G, MSG_G)

    def send_back(place):
        lon = lon_of(place)
        copy_or_keep(w_ref.at[pl.ds(place * MSG_G, MSG_G)], o_ref.at[back_rows], 3, 0, (lon, p))

    loads[0].wait()
    gather_rows(t_ref, sb_ref)
    pl.semaphore_wait(barrier, LON - 1 + LAT - 1)
    lax.fori_loop(1, LON, send_grid, 0)
    pltpu.make_async_copy(
        sb_ref.at[pl.ds(q * MSG_G, MSG_G)], r_ref.at[pl.ds(here * SLOT_G, MSG_G)], recv_sem.at[0, here // 8]
    ).start()

    def tell(n, _):
        pl.semaphore_signal(ready_sem, inc=1, device_id=(q, (p + n) % LAT), device_id_type=MESH)
        return 0

    lax.fori_loop(1, LAT, tell, 0)

    loads[1].wait()
    legendre_tables(q, start_ref, slope_ref, lag_ref, trig_ref, p_ref)
    fsum_ref[...] = jnp.zeros_like(fsum_ref)
    isum_ref[...] = jnp.zeros_like(isum_ref)
    loads[2].wait()
    loads[3].wait()

    def grid_group(step):
        group = (here // 8 + 4 - step) % 4
        wait(r_ref, group * 8 * SLOT_G, 8 * MSG_G, recv_sem.at[0, group])
        forward_operand(group, r_ref, x_ref)
        return group

    def forward_step(step, _):
        add_products(grid_group(step), x_ref, fh_ref, fl_ref, fsum_ref)
        return 0

    lax.fori_loop(0, 3, forward_step, 0)
    group = grid_group(3)
    pl.semaphore_wait(ready_sem, LAT - 1)
    forward_blocks(q, south, group, x_ref, fh_ref, fl_ref, fsum_ref, block_ref, m_ref, send_waves)
    for load in loads[4:]:
        load.wait()
    wait(sb_ref, 0, (LON - 1) * MSG_G, send_sem.at[0])
    wait(g_ref, 0, 32 * MSG_C, recv_sem.at[1, 0])
    analysis(g_ref, trig_ref, eo_ref, p_ref, a_ref)
    update(q, stiff_ref[p], damp_ref[p], state_ref, a_ref, ns_ref, st_ref)
    synthesis(p_ref, st_ref, h_ref)
    lax.fori_loop(0, 32, send_rows, 0)

    def wait_sent(ref, own, stage):
        @pl.when(own)
        def _():
            wait(ref, 0, 31 * MSG_C, send_sem.at[stage])

        @pl.when(jnp.logical_not(own))
        def _():
            wait(ref, 0, 32 * MSG_C, send_sem.at[stage])

    wait_sent(m_ref, owned == p, 1)

    def waves_group(step):
        group = (back_slot // 8 + 4 - step) % 4
        wait(cp_ref, group * 8 * SLOT_C, 8 * MSG_C, recv_sem.at[2, group])
        inverse_operand(group, south, cp_ref, y_ref)
        return group

    def inverse_step(step, _):
        add_products(waves_group(step), y_ref, ih_ref, il_ref, isum_ref)
        return 0

    lax.fori_loop(0, 3, inverse_step, 0)
    inverse_blocks(q, waves_group(3), y_ref, ih_ref, il_ref, isum_ref, block_ref, w_ref, send_back)
    wait_sent(h_ref, back_mode == p, 2)
    wait(o_ref, 0, LON * MSG_G, recv_sem.at[3, 0])
    wait(w_ref, 0, (LON - 1) * MSG_G, send_sem.at[3])


def place_kernel(ns_ref, o_ref, ns_any, out_any, ns_sem, out_sem):
    state_copy = pltpu.make_async_copy(ns_ref, ns_any, ns_sem)
    state_copy.start()

    def body(d, _):
        for f in range(3):
            pltpu.make_async_copy(
                o_ref.at[pl.ds(d * MSG_G + f * 9, 9)],
                out_any.at[pl.ds((f * MODES + d // 2) * 18 + d % 2 * 9, 9)],
                out_sem,
            ).start()
        return 0

    lax.fori_loop(0, LON, body, 0)
    pltpu.make_async_copy(o_ref, out_any, out_sem).wait()
    state_copy.wait()


def body(tendency, state, stiffness, damping):
    rows = LON * MSG_G
    vmem = pl.BlockSpec(memory_space=pltpu.VMEM)
    anywhere = pl.BlockSpec(memory_space=pl.ANY)
    shapes = (jax.ShapeDtypeStruct((FR * MDEV, WAVES), F32), jax.ShapeDtypeStruct((rows, 128), F32))
    new_state, new_fields = pl.pallas_call(
        kernel,
        out_shape=shapes,
        in_specs=[anywhere] * 9,
        out_specs=(vmem, vmem),
        scratch_shapes=[
            pltpu.VMEM((rows, 128), F32),
            pltpu.VMEM((FR * MDEV, WAVES), F32),
            pltpu.VMEM((LON, 128), F32),
            pltpu.SMEM((MODES,), F32),
            pltpu.SMEM((MODES,), F32),
            pltpu.VMEM((64 * LON, 2 * WAVES), BF16),
            pltpu.VMEM((64 * LON, 2 * WAVES), BF16),
            pltpu.VMEM((2 * WAVES, 64 * LON), BF16),
            pltpu.VMEM((2 * WAVES, 64 * LON), BF16),
            pltpu.VMEM((rows, 128), F32),
            pltpu.VMEM((LON * SLOT_G, 128), F32),
            pltpu.VMEM((256, 512), BF16),
            pltpu.VMEM((128, 2 * WAVES), F32),
            pltpu.VMEM((128, 256), F32),
            pltpu.VMEM((32 * MSG_C, 128), F32),
            pltpu.VMEM((32 * MSG_C, 128), F32),
            pltpu.VMEM((FR * PLANE, 128), F32),
            pltpu.VMEM((WAVES, 128), F32),
            pltpu.VMEM((WAVES, 128), F32),
            pltpu.VMEM((ROWS, 128), F32),
            pltpu.VMEM((WAVES // 8 * PLANE, 128), F32),
            pltpu.VMEM((FR * WAVES, 128), F32),
            pltpu.VMEM((FR * WAVES, 128), F32),
            pltpu.VMEM((32 * MSG_C, 128), F32),
            pltpu.VMEM((32 * SLOT_C, 128), F32),
            pltpu.VMEM((256, 256), BF16),
            pltpu.VMEM((128, 64 * LON), F32),
            pltpu.VMEM((rows, 128), F32),
            pltpu.SemaphoreType.DMA((9,)),
            pltpu.SemaphoreType.DMA((4,)),
            pltpu.SemaphoreType.DMA((4, 4)),
            pltpu.SemaphoreType.REGULAR,
        ],
        compiler_params=pltpu.CompilerParams(
            collective_id=0, has_side_effects=True, vmem_limit_bytes=63 * 2**20
        ),
        name="spectral_step",
    )(
        tendency.reshape(rows, 128),
        state.reshape(FR * MDEV, WAVES),
        jnp.asarray(start_constants()),
        stiffness,
        damping,
        *[jnp.asarray(table) for table in fourier_constants()],
    )
    new_state, new_fields = pl.pallas_call(
        place_kernel,
        out_shape=shapes,
        in_specs=[vmem, vmem],
        out_specs=(anywhere, anywhere),
        scratch_shapes=[pltpu.SemaphoreType.DMA, pltpu.SemaphoreType.DMA],
        name="place_rows",
    )(new_state, new_fields)
    return new_state.reshape(state.shape), new_fields.reshape(tendency.shape)


def solution(mesh):
    return jax.shard_map(
        body,
        mesh=mesh,
        in_specs=(P(None, None, "lat", "lon", None), P("lat", None, None, "lon", None), P(), P()),
        out_specs=(P("lat", None, None, "lon", None), P(None, None, "lat", "lon", None)),
        check_vma=False,
    )
```

time: 114 us -> 90.1 us (0.79)
  Pallas kernels: 106 us -> 88.3 us
  local copies, waits for them, and re-layouts: 5.4 us -> 0 us
    pallas_call x1 -> x2, Pallas kernels: 106 us -> 88.3 us  [the longest x1 86.1 us: body(): pl.pallas_call(kernel, out_shape=shapes, in_specs=[anywhere] * 9, out_spe...]
    unnamed x12 -> x0, local copies, waits for them, and re-layouts: 5.4 us -> none
where the time goes in v1:
time: 90.1 us; the launch traced here: 88.9 us
  Pallas kernels  88.3 us (98%)
    pallas_call x1, Pallas kernels, body(): pl.pallas_call(kernel, out_shape=shapes, in_specs=[anywhere] * 9, out_spe...  86.1 us
    pallas_call x1, Pallas kernels, body(): pl.pallas_call(place_kernel, out_shape=shapes, in_specs=[vmem, vmem], out...  2.15 us

profile of v1, /device:TPU:1, one launch (start us, length us, event | category | flops | bytes accessed | tf_op | source)
XLA Modules:
  0.0 88.9 jit_solution(6616270634173626204)
XLA Ops:
  0.6 86.1 %spectral_step.1 = (f32[96,512]{1,0:T(8,128)}, f32[864,128]{1,0:T(8,128)}) custom-call(f32[864,128]{1,0:T(8,128)} %bitcast.4, f32[96,512]{1,0:T(8,128)} %bitcast.5, f32[32,128]{1,0:T(8,128)} %constant.10.clone.start_any, f32[16]{0:T(128)} %stiff_any.1, f32[16]{0:T(128)} %damp_any.1, bf16[2048,1024]{1,0:T(8,128)(2,1)} %constant.11.clone.fh_any, ...), custom_call_target="tpu_custom_call" | custom-call | tf_op jit(solution)/shard_map/spectral_step/pallas_call | solution.py:626
  86.8 2.1 %place_rows.1 = (f32[96,512]{1,0:T(8,128)}, f32[864,128]{1,0:T(8,128)}) custom-call(f32[96,512]{1,0:T(8,128)} %get-tuple-element.6.ns_ref, f32[864,128]{1,0:T(8,128)} %get-tuple-element.7.o_ref), custom_call_target="tpu_custom_call" | custom-call | tf_op jit(solution)/shard_map/place_rows/pallas_call | solution.py:677

commit v2 on v1

--- a/solution.py
+++ b/solution.py
@@ -24,6 +24,10 @@
 SLOT_C = 32
 MSG_C = 18
 FR = 6
+HALF = 8
+QUADS = 17
+LINES = QUADS * 32
+LINES_PAD = 768
 PLANE = 384
 ROWS = 48
 MESH = pl.DeviceIdType.MESH
@@ -54,11 +58,12 @@
     wave = np.arange(WAVES)
     angle = 2.0 * np.pi / NLON * ((lon[:, None] * wave[None, :]) % NLON)
     owners = lon_of(np.arange(LON))
-    cosine = np.where(valid, np.cos(angle), 0.0).reshape(-1, LON, MDEV)[:, owners]
-    sine = np.where(valid, np.sin(angle), 0.0).reshape(-1, LON, MDEV)[:, owners]
-    basis = np.stack([cosine, -sine], axis=2).reshape(LON * 64, 2 * WAVES)
-    factor = np.where(wave == 0, 1.0, 2.0).reshape(LON, 1, MDEV) / WAVES
-    factor = np.broadcast_to(factor[owners], (LON, 2, MDEV)).reshape(2 * WAVES, 1)
+    sets = np.stack([owners, 63 - owners], axis=1)
+    cosine = np.where(valid, np.cos(angle), 0.0).reshape(-1, 64, HALF)[:, sets]
+    sine = np.where(valid, np.sin(angle), 0.0).reshape(-1, 64, HALF)[:, sets]
+    basis = np.stack([cosine, -sine], axis=3).reshape(LON * 64, 2 * WAVES)
+    factor = np.where(wave == 0, 1.0, 2.0).reshape(64, HALF)[sets] / WAVES
+    factor = np.broadcast_to(factor[:, :, None, :], (LON, 2, 2, HALF)).reshape(2 * WAVES, 1)
     return split_constant(basis / NLON) + split_constant(factor * basis.T)
 
 
@@ -69,7 +74,7 @@
         / math.log(2.0)
         for m in range(WAVES)
     ]
-    return np.tile(np.array(start, np.float32).reshape(LON, MDEV), (1, GROUPS))
+    return np.tile(np.array(start, np.float32).reshape(64, HALF), (1, 2 * GROUPS))
 
 
 def lanes(shape):
@@ -134,22 +139,31 @@
     lax.fori_loop(0, LON, body, 0)
 
 
+def set_lines(q):
+    return (64 - q + 3) // 4 * 32
+
+
 def legendre_tables(q, start_ref, slope_ref, lag_ref, trig_ref, p_ref):
-    wave = (lanes((1, 128)) % MDEV + q * MDEV).astype(F32)
+    member = lanes((1, 128)) % HALF
+    waves = ((member + HALF * q).astype(F32), (member + HALF * (63 - q)).astype(F32))
+    split_line = set_lines(q)
 
     def coefficients(block, _):
-        offsets = (lax.broadcasted_iota(jnp.int32, (64, 128), 0) + block * 64).astype(F32)
+        line = lax.broadcasted_iota(jnp.int32, (32, 128), 0) + block * 32
+        second = line >= split_line
+        offsets = jnp.where(second, line - split_line, line).astype(F32)
+        wave = jnp.where(second, waves[1], waves[0])
         degree = wave + offsets
         spacing = jnp.maximum(offsets * (2.0 * wave + offsets), 1.0)
         slope = jnp.sqrt(jnp.maximum(4.0 * degree * degree - 1.0, 0.0) / spacing)
         numerator = (2.0 * degree + 1.0) * (offsets - 1.0) * (degree - 1.0 + wave)
         lag = jnp.sqrt(jnp.maximum(numerator, 0.0) / (jnp.maximum(2.0 * degree - 3.0, 1.0) * spacing))
         first = offsets < 0.5
-        slope_ref[block_rows(block, 64), :] = jnp.where(first, 0.0, slope)
-        lag_ref[block_rows(block, 64), :] = jnp.where(first, 1.0, lag)
-        return 0
-
-    lax.fori_loop(0, WAVES // 64, coefficients, 0)
+        slope_ref[block_rows(block, 32), :] = jnp.where(first, 0.0, slope)
+        lag_ref[block_rows(block, 32), :] = jnp.where(first, 1.0, lag)
+        return 0
+
+    lax.fori_loop(0, QUADS, coefficients, 0)
     row = lax.broadcasted_iota(jnp.int32, (ROWS, 128), 0)
     colat = ((row // 24) * 8 + row % 8) * 24 + (row // 8 % 3) * 8 + lanes((ROWS, 128)) // MDEV
     theta = math.pi * (colat.astype(F32) + 0.5) / NLAT
@@ -158,26 +172,30 @@
     trig_ref[...] = sine * (WAVES * math.pi / NLAT)
     log_sine = jnp.log(sine) * (1.0 / math.log(2.0))
     coarse = jnp.floor(log_sine * 1024.0) * (1.0 / 1024.0)
-    whole = wave * coarse
-    exponent = jnp.floor(whole)
-    fraction = (whole - exponent) + wave * (log_sine - coarse) + start_ref[pl.ds(q, 1), :]
-    lower = -jnp.exp2(fraction)
-    upper = jnp.zeros_like(lower)
-
-    def body(block, carry):
-        upper, lower, exponent = carry
-        growth = jnp.exp2(jnp.maximum(exponent, -140.0))
-        for offset in range(8):
-            k = block * 8 + offset
-            moved = (slope_ref[pl.ds(k, 1), :] * mu) * upper - lag_ref[pl.ds(k, 1), :] * lower
-            upper, lower = moved, upper
-            inside = wave + k.astype(F32) <= WAVES - 1.0
-            p_ref[pl.ds(block * PLANE + offset, ROWS, stride=8), :] = jnp.where(inside, upper * growth, 0.0)
-        big = jnp.maximum(jnp.abs(upper), jnp.abs(lower)) > 2.0**32
-        scale = jnp.where(big, 2.0**-32, 1.0)
-        return upper * scale, lower * scale, exponent + jnp.where(big, 32.0, 0.0)
-
-    lax.fori_loop(0, WAVES // 8, body, (upper, lower, exponent))
+    blocks = split_line // 8
+
+    for which, (begin, end) in enumerate(((0, blocks), (blocks, LINES // 8))):
+        wave = waves[which]
+        whole = wave * coarse
+        exponent = jnp.floor(whole)
+        start = start_ref[pl.ds(63 - q if which else q, 1), :]
+        lower = -jnp.exp2((whole - exponent) + wave * (log_sine - coarse) + start)
+
+        def body(block, carry, begin=begin, wave=wave):
+            upper, lower, exponent = carry
+            growth = jnp.exp2(jnp.maximum(exponent, -140.0))
+            for offset in range(8):
+                line = block * 8 + offset
+                moved = (slope_ref[pl.ds(line, 1), :] * mu) * upper - lag_ref[pl.ds(line, 1), :] * lower
+                upper, lower = moved, upper
+                k = line - begin * 8
+                inside = wave + k.astype(F32) <= WAVES - 1.0
+                p_ref[pl.ds(block * PLANE + offset, ROWS, stride=8), :] = jnp.where(inside, upper * growth, 0.0)
+            big = jnp.maximum(jnp.abs(upper), jnp.abs(lower)) > 2.0**32
+            scale = jnp.where(big, 2.0**-32, 1.0)
+            return upper * scale, lower * scale, exponent + jnp.where(big, 32.0, 0.0)
+
+        lax.fori_loop(begin, end, body, (jnp.zeros_like(lower), lower, exponent))
 
 
 def forward_operand(group, r_ref, x_ref):
@@ -241,97 +259,104 @@
     lax.fori_loop(0, 4, body, 0)
 
 
-def analysis(g_ref, trig_ref, eo_ref, p_ref, a_ref):
+def analysis(q, g_ref, trig_ref, eo_ref, p_ref, a_ref):
     for n in range(2):
         for s in range(3):
             weight = trig_ref[n * 24 + s * 8 : n * 24 + s * 8 + 8, :]
-            for f in range(3):
-                for r in range(2):
-                    north = g_ref[pl.ds(n * 8 * MSG_C + r * 9 + f * 3 + s, 8, stride=MSG_C), :]
-                    south = g_ref[pl.ds((16 + n * 8) * MSG_C + r * 9 + f * 3 + 2 - s, 8, stride=MSG_C), :]
-                    first = (f * 2 + r) * PLANE + (n * 24 + s * 8) * 8
+            for which in range(2):
+                for f in range(3):
+                    line = which * 9 + f * 3
+                    north = g_ref[pl.ds(n * 8 * MSG_C + line + s, 8, stride=MSG_C), :]
+                    south = g_ref[pl.ds((16 + n * 8) * MSG_C + line + 2 - s, 8, stride=MSG_C), :]
+                    first = (which * 3 + f) * PLANE + (n * 24 + s * 8) * 8
                     even, odd = (north + south) * weight, (north - south) * weight
                     for k in range(8):
                         eo_ref[pl.ds(first + k, 8, stride=8), :] = odd if k % 2 else even
 
+    quads = set_lines(q) // 32
+
     def body(quad, _):
+        base = jnp.where(quad >= quads, 3 * PLANE, 0)
+
         def rows(group, sums):
             sums = list(sums)
-            for row in range(8):
-                first = (group * 8 + row) * 8
-                fields = [eo_ref[pl.ds(pl.multiple_of(fr * PLANE + first, 8), 8), :] for fr in range(FR)]
+            for row in range(16):
+                first = (group * 16 + row) * 8
+                fields = [eo_ref[pl.ds(pl.multiple_of(base + f * PLANE + first, 8), 8), :] for f in range(3)]
                 for b in range(4):
                     plane = p_ref[pl.ds(pl.multiple_of((quad * 4 + b) * PLANE + first, 8), 8), :]
-                    for fr in range(FR):
-                        sums[b * FR + fr] = sums[b * FR + fr] + plane * fields[fr]
+                    for f in range(3):
+                        sums[b * 3 + f] = sums[b * 3 + f] + plane * fields[f]
             return tuple(sums)
 
-        sums = lax.fori_loop(0, ROWS // 8, rows, (jnp.zeros((8, 128), F32),) * (4 * FR))
+        sums = lax.fori_loop(0, ROWS // 16, rows, (jnp.zeros((8, 128), F32),) * 12)
         for b in range(4):
-            for fr in range(FR):
-                a_ref[pl.ds(pl.multiple_of(fr * WAVES + (quad * 4 + b) * 8, 8), 8), :] = sums[b * FR + fr]
-        return 0
-
-    lax.fori_loop(0, WAVES // 32, body, 0)
-
-
-def update(q, stiff, damp, state_ref, a_ref, ns_ref, st_ref):
-    wave = (lax.broadcasted_iota(jnp.int32, (MDEV, WAVES), 0) + q * MDEV).astype(F32)
-    degree = wave + lanes((MDEV, WAVES)).astype(F32)
-    ratio = degree * (degree + 1.0) / (WAVES * (WAVES - 1.0))
-    inside = degree <= WAVES - 1.0
-    denominator = 1.0 + stiff * ratio
-    damped = jnp.where(inside, 1.0 / (1.0 + damp * ratio * ratio), 0.0)
-
-    def total(fr):
-        turned = jnp.transpose(a_ref[fr * WAVES : (fr + 1) * WAVES, :])
-        pieces = [turned[16 * n : 16 * n + 16] for n in range(GROUPS)]
-        summed = ((pieces[0] + pieces[1]) + (pieces[2] + pieces[3])) + ((pieces[4] + pieces[5]) + (pieces[6] + pieces[7]))
-        return state_ref[fr * MDEV : (fr + 1) * MDEV, :] + summed
-
-    def put(fr, value):
-        ns_ref[fr * MDEV : (fr + 1) * MDEV, :] = value
-        st_ref[fr * WAVES : (fr + 1) * WAVES, :] = jnp.transpose(jnp.concatenate([value] * GROUPS, axis=0))
-
-    for r in range(2):
-        vorticity, divergence, height = total(r), total(2 + r), total(4 + r)
-        put(r, vorticity * damped)
-        put(2 + r, (divergence + ratio * height) / denominator * damped)
-        put(4 + r, (height - stiff * divergence) / denominator * damped)
-
-
-def synthesis(p_ref, st_ref, h_ref):
+            for f in range(3):
+                a_ref[pl.ds(pl.multiple_of(f * LINES_PAD + (quad * 4 + b) * 8, 8), 8), :] = sums[b * 3 + f]
+        return 0
+
+    lax.fori_loop(0, QUADS, body, 0)
+
+
+def update(q, stiff, damp, state_refs, a_ref, ns_refs, st_ref):
+    for which in range(2):
+        state_ref, ns_ref = state_refs[which], ns_refs[which]
+        size = ns_ref.shape[2]
+        start = pl.multiple_of(set_lines(q) if which else 0 * q, 32)
+        member = lax.broadcasted_iota(jnp.int32, (MDEV, size), 0) % HALF
+        wave = (member + HALF * (63 - q if which else q)).astype(F32)
+        degree = wave + lanes((MDEV, size)).astype(F32)
+        ratio = degree * (degree + 1.0) / (WAVES * (WAVES - 1.0))
+        inside = degree <= WAVES - 1.0
+        denominator = 1.0 + stiff * ratio
+        damped = jnp.where(inside, 1.0 / (1.0 + damp * ratio * ratio), 0.0)
+
+        def total(f):
+            turned = jnp.transpose(a_ref[pl.ds(f * LINES_PAD + start, size), :])
+            pieces = [turned[16 * n : 16 * n + 16] for n in range(GROUPS)]
+            summed = ((pieces[0] + pieces[1]) + (pieces[2] + pieces[3])) + (
+                (pieces[4] + pieces[5]) + (pieces[6] + pieces[7])
+            )
+            old = jnp.concatenate([state_ref[f * 2], state_ref[f * 2 + 1]], axis=0)
+            return jnp.where(inside, old + summed, 0.0)
+
+        def put(f, value):
+            ns_ref[f * 2] = value[0:8]
+            ns_ref[f * 2 + 1] = value[8:16]
+            turned = jnp.transpose(jnp.concatenate([value] * GROUPS, axis=0))
+            st_ref[pl.ds(f * LINES_PAD + start, size), :] = turned
+
+        vorticity, divergence, height = total(0), total(1), total(2)
+        put(0, vorticity * damped)
+        put(1, (divergence + ratio * height) / denominator * damped)
+        put(2, (height - stiff * divergence) / denominator * damped)
+
+
+def synthesis(q, group, p_ref, st_ref, h_ref):
     sign = jnp.where(lax.broadcasted_iota(jnp.int32, (8, 128), 0) % 2 == 0, 1.0, -1.0)
-
-    def body(group, _):
-        n, s = group // 3, group % 3
-        for chunk in range(2):
-
-            def degrees(block, sums):
-                sums = list(sums)
-                for b in range(2):
-                    first = (block * 2 + b) * PLANE + group * 64
-                    values = [
-                        st_ref[pl.ds(pl.multiple_of((chunk * 3 + m) * WAVES + (block * 2 + b) * 8, 8), 8), :]
-                        for m in range(3)
-                    ]
-                    for row in range(8):
-                        plane = p_ref[pl.ds(pl.multiple_of(first + row * 8, 8), 8), :]
-                        for m in range(3):
-                            sums[m * 8 + row] = sums[m * 8 + row] + plane * values[m]
-                return tuple(sums)
-
-            sums = lax.fori_loop(0, WAVES // 16, degrees, (jnp.zeros((8, 128), F32),) * 24)
-            for m in range(3):
-                f, r = divmod(chunk * 3 + m, 2)
-                parts = list(sums[m * 8 : m * 8 + 8])
-                line = r * 9 + f * 3
-                h_ref[pl.ds(n * 8 * MSG_C + line + s, 8, stride=MSG_C), :] = fold_rows(parts)
-                parts = [part * sign for part in parts]
-                h_ref[pl.ds((16 + n * 8) * MSG_C + line + 2 - s, 8, stride=MSG_C), :] = fold_rows(parts)
-        return 0
-
-    lax.fori_loop(0, ROWS // 8, body, 0)
+    quads = set_lines(q) // 32
+    n, s = group // 3, group % 3
+    for which, (begin, end) in enumerate(((0, quads), (quads, QUADS))):
+
+        def degrees(quad, sums):
+            sums = list(sums)
+            for b in range(4):
+                block = quad * 4 + b
+                values = [st_ref[pl.ds(pl.multiple_of(f * LINES_PAD + block * 8, 8), 8), :] for f in range(3)]
+                for row in range(8):
+                    first = block * PLANE + group * 64 + row * 8
+                    plane = p_ref[pl.ds(pl.multiple_of(first, 8), 8), :]
+                    for f in range(3):
+                        sums[f * 8 + row] = sums[f * 8 + row] + plane * values[f]
+            return tuple(sums)
+
+        sums = lax.fori_loop(begin, end, degrees, (jnp.zeros((8, 128), F32),) * 24)
+        for f in range(3):
+            parts = list(sums[f * 8 : f * 8 + 8])
+            line = which * 9 + f * 3
+            h_ref[pl.ds(n * 8 * MSG_C + line + s, 8, stride=MSG_C), :] = fold_rows(parts)
+            parts = [part * sign for part in parts]
+            h_ref[pl.ds((16 + n * 8) * MSG_C + line + 2 - s, 8, stride=MSG_C), :] = fold_rows(parts)
 
 
 def inverse_operand(group, south, cp_ref, y_ref):
@@ -341,18 +366,17 @@
         for a in range(GROUPS):
             row = mirrored(south, a)
             high, low = split(items[a])
-            y_ref[block_rows(row, 16), column * 128 : (column + 1) * 128] = high
-            y_ref[block_rows(row + GROUPS, 16), column * 128 : (column + 1) * 128] = low
-
-
-def inverse_blocks(q, group, y_ref, high_ref, low_ref, sum_ref, block_ref, w_ref, send):
+            y_ref[block_rows(row, 16), block_rows(group * 2 + column, 128)] = high
+            y_ref[block_rows(row + GROUPS, 16), block_rows(group * 2 + column, 128)] = low
+
+
+def inverse_blocks(q, y_ref, high_ref, low_ref, block_ref, w_ref, send):
     lane = lanes((16, 128))
-    rows = block_rows(group, y_ref.shape[1])
 
     def body(step, _):
         block = (step + q % 4 * 2) % 8
         columns = block_rows(block, 256)
-        block_ref[...] = sum_ref[:, columns] + product(y_ref, high_ref, low_ref, rows, columns)
+        block_ref[...] = product(y_ref, high_ref, low_ref, slice(None), columns)
         for index in range(4):
             half, par = divmod(index, 2)
             owner = block * 4 + index
@@ -393,7 +417,10 @@
     ns_ref,
     o_ref,
     t_ref,
-    state_ref,
+    low_state_ref,
+    high_state_ref,
+    low_new_ref,
+    high_new_ref,
     start_ref,
     stiff_ref,
     damp_ref,
@@ -418,7 +445,6 @@
     h_ref,
     cp_ref,
     y_ref,
-    isum_ref,
     w_ref,
     load_sem,
     send_sem,
@@ -435,6 +461,7 @@
     back_half = q % 2
     back_slot = slot_of(p * 2 + back_half)
 
+    ns_ref[...] = jnp.zeros_like(ns_ref)
     barrier = pltpu.get_barrier_semaphore()
 
     def greet_lon(n, _):
@@ -456,7 +483,6 @@
                 (start_any, start_ref),
                 (fh_any, fh_ref),
                 (fl_any, fl_ref),
-                (state_any, state_ref),
                 (stiff_any, stiff_ref),
                 (damp_any, damp_ref),
                 (ih_any, ih_ref),
@@ -472,7 +498,7 @@
             src_ref=source,
             dst_ref=target,
             send_sem=send_sem.at[stage],
-            recv_sem=recv_sem.at[stage, group],
+            recv_sem=recv_sem.at[4 if stage in (4, 5) else 5 if stage > 5 else stage, group],
             device_id=peer,
             device_id_type=MESH,
         )
@@ -508,8 +534,9 @@
             (lon_of(place), owned),
         )
 
-    def send_rows(n, _):
-        slot = (here // 8 + n // 8) % 4 * 8 + (here + n) % 8
+    def send_rows(n, part):
+        index = (here // 8 * 4 + n) % 16
+        slot = index // 8 * 16 + part * 8 + index % 8
         source = slot_of(slot)
         lat = source // 2
         lon = (p // 2 + lat // 2 + lat % 2 * 4) % 8 * 4 + p % 2 * 2 + source % 2
@@ -520,13 +547,79 @@
             here // 8,
             (lon, lat),
         )
-        return 0
-
-    back_rows = pl.ds((back_mode * 2 + back_half) * MSG_G, MSG_G)
+        return part
 
     def send_back(place):
-        lon = lon_of(place)
-        copy_or_keep(w_ref.at[pl.ds(place * MSG_G, MSG_G)], o_ref.at[back_rows], 3, 0, (lon, p))
+        for f in range(3):
+            copy_or_keep(
+                w_ref.at[pl.ds(place * MSG_G + f * 9, 9)],
+                o_ref.at[pl.ds((f * MODES + back_mode) * 18 + back_half * 9, 9)],
+                3,
+                0,
+                (lon_of(place), p),
+            )
+
+    def state_copies(index):
+        rows = pl.ds(index * HALF, HALF)
+        low = (
+            (2 * q + index, p),
+            lambda: copy(state_any.at[:, rows, :], low_state_ref, 4 + index, 0, (2 * q + index, p)),
+            lambda: pltpu.make_async_copy(state_any.at[:, rows, :], low_state_ref, recv_sem.at[4, 0]),
+        )
+        worker = 63 - 2 * q - index
+        high = (
+            (worker, p),
+            lambda: copy(state_any.at[:, rows, 0:256], high_state_ref, 4 + index, 1, (worker, p)),
+            lambda: pltpu.make_async_copy(state_any.at[:, rows, 0:256], high_state_ref, recv_sem.at[4, 1]),
+        )
+        return low, high
+
+    def new_copies():
+        low_rows = pl.ds(q % 2 * HALF, HALF)
+        high_rows = pl.ds((63 - q) % 2 * HALF, HALF)
+        owner = (63 - q) // 2
+        low = (
+            q // 2,
+            lambda: copy(low_new_ref, ns_ref.at[:, low_rows, :], 6, 0, (q // 2, p)),
+            lambda: pltpu.make_async_copy(low_new_ref, ns_ref.at[:, low_rows, :], recv_sem.at[5, 0]),
+        )
+        high = (
+            owner,
+            lambda: copy(high_new_ref, ns_ref.at[:, high_rows, 0:256], 7, 0, (owner, p)),
+            lambda: pltpu.make_async_copy(high_new_ref, ns_ref.at[:, high_rows, 0:256], recv_sem.at[5, 0]),
+        )
+        return low, high
+
+    def each_state_copy(act):
+        for index in range(2):
+            low, high = state_copies(index)
+            for (peer, remote, local), mine in ((low, q < 16), (high, q >= 16)):
+
+                @pl.when(jnp.logical_and(mine, peer[0] != q))
+                def _():
+                    act(remote, False)
+
+                @pl.when(jnp.logical_and(mine, peer[0] == q))
+                def _():
+                    act(local, True)
+
+    def each_new_copy(act):
+        for peer, remote, local in new_copies():
+
+            @pl.when(peer != q)
+            def _():
+                act(remote, False)
+
+            @pl.when(peer == q)
+            def _():
+                act(local, True)
+
+    def begin(item, own):
+        item().start()
+
+    def sent(item, own):
+        if not own:
+            item().wait_send()
 
     loads[0].wait()
     gather_rows(t_ref, sb_ref)
@@ -544,8 +637,8 @@
 
     loads[1].wait()
     legendre_tables(q, start_ref, slope_ref, lag_ref, trig_ref, p_ref)
+    each_state_copy(begin)
     fsum_ref[...] = jnp.zeros_like(fsum_ref)
-    isum_ref[...] = jnp.zeros_like(isum_ref)
     loads[2].wait()
     loads[3].wait()
 
@@ -567,10 +660,27 @@
         load.wait()
     wait(sb_ref, 0, (LON - 1) * MSG_G, send_sem.at[0])
     wait(g_ref, 0, 32 * MSG_C, recv_sem.at[1, 0])
-    analysis(g_ref, trig_ref, eo_ref, p_ref, a_ref)
-    update(q, stiff_ref[p], damp_ref[p], state_ref, a_ref, ns_ref, st_ref)
-    synthesis(p_ref, st_ref, h_ref)
-    lax.fori_loop(0, 32, send_rows, 0)
+    analysis(q, g_ref, trig_ref, eo_ref, p_ref, a_ref)
+    each_state_copy(sent)
+    pltpu.make_async_copy(low_state_ref, low_state_ref, recv_sem.at[4, 0]).wait()
+    pltpu.make_async_copy(high_state_ref, high_state_ref, recv_sem.at[4, 1]).wait()
+    update(
+        q,
+        stiff_ref[p],
+        damp_ref[p],
+        (low_state_ref, high_state_ref),
+        a_ref,
+        (low_new_ref, high_new_ref),
+        st_ref,
+    )
+    each_new_copy(begin)
+
+    def synthesize(part, _):
+        lax.fori_loop(0, 3, lambda s, _: (synthesis(q, part * 3 + s, p_ref, st_ref, h_ref), 0)[1], 0)
+        lax.fori_loop(0, 16, send_rows, part)
+        return 0
+
+    lax.fori_loop(0, 2, synthesize, 0)
 
     def wait_sent(ref, own, stage):
         @pl.when(own)
@@ -583,46 +693,35 @@
 
     wait_sent(m_ref, owned == p, 1)
 
-    def waves_group(step):
+    def waves_group(step, _):
         group = (back_slot // 8 + 4 - step) % 4
         wait(cp_ref, group * 8 * SLOT_C, 8 * MSG_C, recv_sem.at[2, group])
         inverse_operand(group, south, cp_ref, y_ref)
-        return group
-
-    def inverse_step(step, _):
-        add_products(waves_group(step), y_ref, ih_ref, il_ref, isum_ref)
-        return 0
-
-    lax.fori_loop(0, 3, inverse_step, 0)
-    inverse_blocks(q, waves_group(3), y_ref, ih_ref, il_ref, isum_ref, block_ref, w_ref, send_back)
+        return 0
+
+    lax.fori_loop(0, 4, waves_group, 0)
+    inverse_blocks(q, y_ref, ih_ref, il_ref, block_ref, w_ref, send_back)
     wait_sent(h_ref, back_mode == p, 2)
+    each_new_copy(sent)
+
+    @pl.when(q < 16)
+    def _():
+        pltpu.make_async_copy(ns_ref, ns_ref, recv_sem.at[5, 0]).wait()
+
+    @pl.when(q >= 16)
+    def _():
+        part = ns_ref.at[:, :, 0:256]
+        pltpu.make_async_copy(part, part, recv_sem.at[5, 0]).wait()
+
     wait(o_ref, 0, LON * MSG_G, recv_sem.at[3, 0])
     wait(w_ref, 0, (LON - 1) * MSG_G, send_sem.at[3])
-
-
-def place_kernel(ns_ref, o_ref, ns_any, out_any, ns_sem, out_sem):
-    state_copy = pltpu.make_async_copy(ns_ref, ns_any, ns_sem)
-    state_copy.start()
-
-    def body(d, _):
-        for f in range(3):
-            pltpu.make_async_copy(
-                o_ref.at[pl.ds(d * MSG_G + f * 9, 9)],
-                out_any.at[pl.ds((f * MODES + d // 2) * 18 + d % 2 * 9, 9)],
-                out_sem,
-            ).start()
-        return 0
-
-    lax.fori_loop(0, LON, body, 0)
-    pltpu.make_async_copy(o_ref, out_any, out_sem).wait()
-    state_copy.wait()
 
 
 def body(tendency, state, stiffness, damping):
     rows = LON * MSG_G
     vmem = pl.BlockSpec(memory_space=pltpu.VMEM)
     anywhere = pl.BlockSpec(memory_space=pl.ANY)
-    shapes = (jax.ShapeDtypeStruct((FR * MDEV, WAVES), F32), jax.ShapeDtypeStruct((rows, 128), F32))
+    shapes = (jax.ShapeDtypeStruct((FR, MDEV, WAVES), F32), jax.ShapeDtypeStruct((rows, 128), F32))
     new_state, new_fields = pl.pallas_call(
         kernel,
         out_shape=shapes,
@@ -630,8 +729,11 @@
         out_specs=(vmem, vmem),
         scratch_shapes=[
             pltpu.VMEM((rows, 128), F32),
-            pltpu.VMEM((FR * MDEV, WAVES), F32),
-            pltpu.VMEM((LON, 128), F32),
+            pltpu.VMEM((FR, HALF, WAVES), F32),
+            pltpu.VMEM((FR, HALF, 256), F32),
+            pltpu.VMEM((FR, HALF, WAVES), F32),
+            pltpu.VMEM((FR, HALF, 256), F32),
+            pltpu.VMEM((64, 128), F32),
             pltpu.SMEM((MODES,), F32),
             pltpu.SMEM((MODES,), F32),
             pltpu.VMEM((64 * LON, 2 * WAVES), BF16),
@@ -646,20 +748,19 @@
             pltpu.VMEM((32 * MSG_C, 128), F32),
             pltpu.VMEM((32 * MSG_C, 128), F32),
             pltpu.VMEM((FR * PLANE, 128), F32),
-            pltpu.VMEM((WAVES, 128), F32),
-            pltpu.VMEM((WAVES, 128), F32),
+            pltpu.VMEM((LINES, 128), F32),
+            pltpu.VMEM((LINES, 128), F32),
             pltpu.VMEM((ROWS, 128), F32),
-            pltpu.VMEM((WAVES // 8 * PLANE, 128), F32),
-            pltpu.VMEM((FR * WAVES, 128), F32),
-            pltpu.VMEM((FR * WAVES, 128), F32),
+            pltpu.VMEM((LINES // 8 * PLANE, 128), F32),
+            pltpu.VMEM((3 * LINES_PAD, 128), F32),
+            pltpu.VMEM((3 * LINES_PAD, 128), F32),
             pltpu.VMEM((32 * MSG_C, 128), F32),
             pltpu.VMEM((32 * SLOT_C, 128), F32),
-            pltpu.VMEM((256, 256), BF16),
-            pltpu.VMEM((128, 64 * LON), F32),
+            pltpu.VMEM((256, 2 * WAVES), BF16),
             pltpu.VMEM((rows, 128), F32),
-            pltpu.SemaphoreType.DMA((9,)),
-            pltpu.SemaphoreType.DMA((4,)),
-            pltpu.SemaphoreType.DMA((4, 4)),
+            pltpu.SemaphoreType.DMA((8,)),
+            pltpu.SemaphoreType.DMA((8,)),
+            pltpu.SemaphoreType.DMA((6, 4)),
             pltpu.SemaphoreType.REGULAR,
         ],
         compiler_params=pltpu.CompilerParams(
@@ -668,20 +769,12 @@
         name="spectral_step",
     )(
         tendency.reshape(rows, 128),
-        state.reshape(FR * MDEV, WAVES),
+        state.reshape(FR, MDEV, WAVES),
         jnp.asarray(start_constants()),
         stiffness,
         damping,
         *[jnp.asarray(table) for table in fourier_constants()],
     )
-    new_state, new_fields = pl.pallas_call(
-        place_kernel,
-        out_shape=shapes,
-        in_specs=[vmem, vmem],
-        out_specs=(anywhere, anywhere),
-        scratch_shapes=[pltpu.SemaphoreType.DMA, pltpu.SemaphoreType.DMA],
-        name="place_rows",
-    )(new_state, new_fields)
     return new_state.reshape(state.shape), new_fields.reshape(tendency.shape)
 
 

time: 90.1 us -> 80.6 us (0.89)
  Pallas kernels: 88.3 us -> 76 us
  local copies, waits for them, and re-layouts: 0 us -> 3.43 us
    pallas_call x1, Pallas kernels: 86.1 us -> 76 us  [body(): pl.pallas_call(kernel, out_shape=shapes, in_specs=[anywhere] * 9, out_spe...]
    unnamed x0 -> x2, local copies, waits for them, and re-layouts: none -> 3.43 us
    pallas_call x1 -> x0, Pallas kernels: 2.15 us -> none  [body(): pl.pallas_call(place_kernel, out_shape=shapes, in_specs=[vmem, vmem], out...]
where the time goes in v2:
time: 80.6 us; the launch traced here: 80.1 us
  Pallas kernels  76 us (94%)
  local copies, waits for them, and re-layouts  3.43 us (4%)
    pallas_call x1, Pallas kernels, body(): pl.pallas_call(kernel, out_shape=shapes, in_specs=[anywhere] * 9, out_spe...  76 us
    unnamed x2, local copies, waits for them, and re-layouts  3.43 us

profile of v2, /device:TPU:1, one launch (start us, length us, event | category | flops | bytes accessed | tf_op | source)
XLA Modules:
  0.0 80.1 jit_solution(14535086745094656335)
XLA Ops:
  0.6 76.0 %spectral_step.1 = (f32[6,16,512]{2,1,0:T(8,128)}, f32[864,128]{1,0:T(8,128)}) custom-call(f32[864,128]{1,0:T(8,128)} %bitcast.4, f32[6,16,512]{2,1,0:T(8,128)} %bitcast.6, f32[64,128]{1,0:T(8,128)} %constant.10.clone.start_any, f32[16]{0:T(128)} %stiff_any.1, f32[16]{0:T(128)} %damp_any.1, bf16[2048,1024]{1,0:T(8,128)(2,1)} %constant.11.clone.fh_any, ...), custom_call_target="tpu_custom_call" | custom-call | tf_op jit(solution)/shard_map/spectral_step/pallas_call | solution.py:725
  76.6 1.6 %copy.14 = f32[1,3,2,16,512]{4,3,2,1,0:T(8,128)} copy(f32[1,3,2,16,512]{4,3,2,1,0:T(8,128)} %bitcast.7) | data formatting | bytes 393216
  78.2 1.8 %copy.15 = f32[3,16,1,1,2304]{4,3,2,1,0:T(1,128)} copy(f32[3,16,1,1,2304]{4,3,2,1,0:T(1,128)} %bitcast.5) | data formatting | bytes 884736

commit v3 on v2

--- a/solution.py
+++ b/solution.py
@@ -242,12 +242,13 @@
     rows = block_rows(group, x_ref.shape[1])
 
     def body(step, _):
-        block = (step + q % 4) % 4
+        block = (q + turn(step)) % 4
         columns = block_rows(block, 256)
         block_ref[...] = sum_ref[:, columns] + product(x_ref, high_ref, low_ref, rows, columns)
-        for half in range(2):
+        for order in range(2):
+            half = jnp.where(q // 4 < 4, 1 - order, order)
             items = swap_groups(
-                [block_ref[block_rows(mirrored(south, a), 16), half * 128 : (half + 1) * 128] for a in range(GROUPS)]
+                [block_ref[block_rows(mirrored(south, a), 16), block_rows(half, 128)] for a in range(GROUPS)]
             )
             for group in range(GROUPS):
                 owner = block * 8 + half * 4 + group // 2
@@ -374,7 +375,7 @@
     lane = lanes((16, 128))
 
     def body(step, _):
-        block = (step + q % 4 * 2) % 8
+        block = (q + turn(step // 2)) % 4 * 2 + jnp.where(q // 4 < 4, 1 - step % 2, step % 2)
         columns = block_rows(block, 256)
         block_ref[...] = product(y_ref, high_ref, low_ref, slice(None), columns)
         for index in range(4):
@@ -400,6 +401,14 @@
     lax.fori_loop(0, 8, body, 0)
 
 
+def far_first(y, n):
+    return (y + jnp.where(n % 2 == 0, 4 - n // 2, 4 + (n + 1) // 2)) % 8
+
+
+def turn(step):
+    return jnp.where(step == 0, 2, jnp.where(step == 1, 1, jnp.where(step == 2, 3, 0)))
+
+
 def slot_of(source):
     return jnp.where(source < 16, source, 47 - source)
 
@@ -421,6 +430,7 @@
     high_state_ref,
     low_new_ref,
     high_new_ref,
+    zero_ref,
     start_ref,
     stiff_ref,
     damp_ref,
@@ -461,7 +471,13 @@
     back_half = q % 2
     back_slot = slot_of(p * 2 + back_half)
 
-    ns_ref[...] = jnp.zeros_like(ns_ref)
+    zero_copy = pltpu.make_async_copy(zero_ref, ns_ref.at[:, :, 256:512], load_sem.at[8])
+
+    @pl.when(q >= 16)
+    def _():
+        zero_ref[...] = jnp.zeros_like(zero_ref)
+        zero_copy.start()
+
     barrier = pltpu.get_barrier_semaphore()
 
     def greet_lon(n, _):
@@ -520,7 +536,7 @@
         pltpu.make_async_copy(part, part, sem).wait()
 
     def send_grid(n, _):
-        place = (here // 8 + n // 8) % 4 * 8 + (here + n) % 8
+        place = (here // 8 + turn(n // 8)) % 4 * 8 + far_first(here % 8, n % 8)
         lon = lon_of(place)
         copy(sb_ref.at[pl.ds(lon * MSG_G, MSG_G)], r_ref.at[pl.ds(here * SLOT_G, MSG_G)], 0, here // 8, (lon, p)).start()
         return 0
@@ -624,7 +640,7 @@
     loads[0].wait()
     gather_rows(t_ref, sb_ref)
     pl.semaphore_wait(barrier, LON - 1 + LAT - 1)
-    lax.fori_loop(1, LON, send_grid, 0)
+    lax.fori_loop(0, LON - 1, send_grid, 0)
     pltpu.make_async_copy(
         sb_ref.at[pl.ds(q * MSG_G, MSG_G)], r_ref.at[pl.ds(here * SLOT_G, MSG_G)], recv_sem.at[0, here // 8]
     ).start()
@@ -643,7 +659,7 @@
     loads[3].wait()
 
     def grid_group(step):
-        group = (here // 8 + 4 - step) % 4
+        group = (here // 8 + 4 - turn(step)) % 4
         wait(r_ref, group * 8 * SLOT_G, 8 * MSG_G, recv_sem.at[0, group])
         forward_operand(group, r_ref, x_ref)
         return group
@@ -710,11 +726,23 @@
 
     @pl.when(q >= 16)
     def _():
+        zero_copy.wait()
         part = ns_ref.at[:, :, 0:256]
         pltpu.make_async_copy(part, part, recv_sem.at[5, 0]).wait()
 
     wait(o_ref, 0, LON * MSG_G, recv_sem.at[3, 0])
     wait(w_ref, 0, (LON - 1) * MSG_G, send_sem.at[3])
+
+
+def result_kernel(ns_ref, o_ref, new_state_any, new_fields_any, sem):
+    copies = [
+        pltpu.make_async_copy(source, target, sem.at[index])
+        for index, (source, target) in enumerate(((ns_ref, new_state_any), (o_ref, new_fields_any)))
+    ]
+    for item in copies:
+        item.start()
+    for item in copies:
+        item.wait()
 
 
 def body(tendency, state, stiffness, damping):
@@ -733,6 +761,7 @@
             pltpu.VMEM((FR, HALF, 256), F32),
             pltpu.VMEM((FR, HALF, WAVES), F32),
             pltpu.VMEM((FR, HALF, 256), F32),
+            pltpu.VMEM((FR, MDEV, 256), F32),
             pltpu.VMEM((64, 128), F32),
             pltpu.SMEM((MODES,), F32),
             pltpu.SMEM((MODES,), F32),
@@ -758,13 +787,13 @@
             pltpu.VMEM((32 * SLOT_C, 128), F32),
             pltpu.VMEM((256, 2 * WAVES), BF16),
             pltpu.VMEM((rows, 128), F32),
-            pltpu.SemaphoreType.DMA((8,)),
+            pltpu.SemaphoreType.DMA((9,)),
             pltpu.SemaphoreType.DMA((8,)),
             pltpu.SemaphoreType.DMA((6, 4)),
             pltpu.SemaphoreType.REGULAR,
         ],
         compiler_params=pltpu.CompilerParams(
-            collective_id=0, has_side_effects=True, vmem_limit_bytes=63 * 2**20
+            collective_id=0, has_side_effects=True, vmem_limit_bytes=60 * 2**20
         ),
         name="spectral_step",
     )(
@@ -775,6 +804,14 @@
         damping,
         *[jnp.asarray(table) for table in fourier_constants()],
     )
+    new_state, new_fields = pl.pallas_call(
+        result_kernel,
+        out_shape=shapes,
+        in_specs=[vmem, vmem],
+        out_specs=(anywhere, anywhere),
+        scratch_shapes=[pltpu.SemaphoreType.DMA((2,))],
+        name="results",
+    )(new_state, new_fields)
     return new_state.reshape(state.shape), new_fields.reshape(tendency.shape)
 
 

time: 80.6 us -> 77.7 us (0.964)
  the two profiles are of different devices: /device:TPU:1 before, /device:TPU:129 now
where the time goes in v3:
time: 77.7 us; the launch traced here: 77.5 us
  Pallas kernels  76.9 us (99%)
    pallas_call x1, Pallas kernels, body(): pl.pallas_call(kernel, out_shape=shapes, in_specs=[anywhere] * 9, out_spe...  74.9 us
    pallas_call x1, Pallas kernels, body(): pl.pallas_call(result_kernel, out_shape=shapes, in_specs=[vmem, vmem], ou...  1.96 us

profile of v3, /device:TPU:129, one launch (start us, length us, event | category | flops | bytes accessed | tf_op | source)
XLA Modules:
  0.0 77.5 jit_solution(3552458276523226466)
XLA Ops:
  0.6 74.9 %spectral_step.1 = (f32[6,16,512]{2,1,0:T(8,128)}, f32[864,128]{1,0:T(8,128)}) custom-call(f32[864,128]{1,0:T(8,128)} %bitcast.4, f32[6,16,512]{2,1,0:T(8,128)} %bitcast.5, f32[64,128]{1,0:T(8,128)} %constant.10.clone.start_any, f32[16]{0:T(128)} %stiff_any.1, f32[16]{0:T(128)} %damp_any.1, bf16[2048,1024]{1,0:T(8,128)(2,1)} %constant.11.clone.fh_any, ...), custom_call_target="tpu_custom_call" | custom-call | tf_op jit(solution)/shard_map/spectral_step/pallas_call | solution.py:753
  75.6 2.0 %results.1 = (f32[6,16,512]{2,1,0:T(8,128)}, f32[864,128]{1,0:T(8,128)}) custom-call(f32[6,16,512]{2,1,0:T(8,128)} %get-tuple-element.6.ns_ref, f32[864,128]{1,0:T(8,128)} %get-tuple-element.7.o_ref), custom_call_target="tpu_custom_call" | custom-call | tf_op jit(solution)/shard_map/results/pallas_call | solution.py:807

commit v4 on v3

--- a/solution.py
+++ b/solution.py
@@ -58,7 +58,8 @@
     wave = np.arange(WAVES)
     angle = 2.0 * np.pi / NLON * ((lon[:, None] * wave[None, :]) % NLON)
     owners = lon_of(np.arange(LON))
-    sets = np.stack([owners, 63 - owners], axis=1)
+    first = np.where(owners < LON // 2, 2 * owners, 63 - 2 * owners)
+    sets = np.stack([first, 63 - first], axis=1)
     cosine = np.where(valid, np.cos(angle), 0.0).reshape(-1, 64, HALF)[:, sets]
     sine = np.where(valid, np.sin(angle), 0.0).reshape(-1, 64, HALF)[:, sets]
     basis = np.stack([cosine, -sine], axis=3).reshape(LON * 64, 2 * WAVES)
@@ -103,17 +104,18 @@
     for index in range(4):
         x, y = parts[index], parts[index + 4]
         four.append(jnp.where(upper, x, y) + pltpu.roll(jnp.where(upper, y, x), 4, 0))
-    for step in (2, 1):
-        keep = (row & step) == 0
-        four = [
-            jnp.where(
-                keep,
-                four[index] + pltpu.roll(four[index], 8 - step, 0),
-                four[index + step] + pltpu.roll(four[index + step], step, 0),
-            )
-            for index in range(step)
-        ]
-    return four[0]
+    keep = (row & 2) == 0
+    a, b = [
+        jnp.where(
+            keep,
+            four[index] + pltpu.roll(four[index], 6, 0),
+            four[index + 2] + pltpu.roll(four[index + 2], 2, 0),
+        )
+        for index in range(2)
+    ]
+    keep = (row & 1) == 0
+    after, before = pltpu.roll(a, 7, 0), pltpu.roll(b, 1, 0)
+    return jnp.where(keep, a + after, before + b), jnp.where(keep, a - after, before - b)
 
 
 def split(x):
@@ -139,14 +141,14 @@
     lax.fori_loop(0, LON, body, 0)
 
 
-def set_lines(q):
-    return (64 - q + 3) // 4 * 32
-
-
-def legendre_tables(q, start_ref, slope_ref, lag_ref, trig_ref, p_ref):
+def set_lines(g):
+    return (64 - g + 3) // 4 * 32
+
+
+def legendre_tables(g, start_ref, slope_ref, lag_ref, trig_ref, p_ref):
     member = lanes((1, 128)) % HALF
-    waves = ((member + HALF * q).astype(F32), (member + HALF * (63 - q)).astype(F32))
-    split_line = set_lines(q)
+    waves = ((member + HALF * g).astype(F32), (member + HALF * (63 - g)).astype(F32))
+    split_line = set_lines(g)
 
     def coefficients(block, _):
         line = lax.broadcasted_iota(jnp.int32, (32, 128), 0) + block * 32
@@ -178,7 +180,7 @@
         wave = waves[which]
         whole = wave * coarse
         exponent = jnp.floor(whole)
-        start = start_ref[pl.ds(63 - q if which else q, 1), :]
+        start = start_ref[pl.ds(63 - g if which else g, 1), :]
         lower = -jnp.exp2((whole - exponent) + wave * (log_sine - coarse) + start)
 
         def body(block, carry, begin=begin, wave=wave):
@@ -260,7 +262,7 @@
     lax.fori_loop(0, 4, body, 0)
 
 
-def analysis(q, g_ref, trig_ref, eo_ref, p_ref, a_ref):
+def analysis(g, g_ref, trig_ref, eo_ref, p_ref, a_ref):
     for n in range(2):
         for s in range(3):
             weight = trig_ref[n * 24 + s * 8 : n * 24 + s * 8 + 8, :]
@@ -274,7 +276,7 @@
                     for k in range(8):
                         eo_ref[pl.ds(first + k, 8, stride=8), :] = odd if k % 2 else even
 
-    quads = set_lines(q) // 32
+    quads = set_lines(g) // 32
 
     def body(quad, _):
         base = jnp.where(quad >= quads, 3 * PLANE, 0)
@@ -299,13 +301,13 @@
     lax.fori_loop(0, QUADS, body, 0)
 
 
-def update(q, stiff, damp, state_refs, a_ref, ns_refs, st_ref):
+def update(g, stiff, damp, state_refs, a_ref, ns_refs, st_ref):
     for which in range(2):
         state_ref, ns_ref = state_refs[which], ns_refs[which]
         size = ns_ref.shape[2]
-        start = pl.multiple_of(set_lines(q) if which else 0 * q, 32)
+        start = pl.multiple_of(set_lines(g) if which else 0 * g, 32)
         member = lax.broadcasted_iota(jnp.int32, (MDEV, size), 0) % HALF
-        wave = (member + HALF * (63 - q if which else q)).astype(F32)
+        wave = (member + HALF * (63 - g if which else g)).astype(F32)
         degree = wave + lanes((MDEV, size)).astype(F32)
         ratio = degree * (degree + 1.0) / (WAVES * (WAVES - 1.0))
         inside = degree <= WAVES - 1.0
@@ -333,31 +335,30 @@
         put(2, (height - stiff * divergence) / denominator * damped)
 
 
-def synthesis(q, group, p_ref, st_ref, h_ref):
-    sign = jnp.where(lax.broadcasted_iota(jnp.int32, (8, 128), 0) % 2 == 0, 1.0, -1.0)
-    quads = set_lines(q) // 32
+def synthesis(g, group, p_ref, st_ref, h_ref):
+    quads = set_lines(g) // 32
     n, s = group // 3, group % 3
-    for which, (begin, end) in enumerate(((0, quads), (quads, QUADS))):
-
-        def degrees(quad, sums):
-            sums = list(sums)
-            for b in range(4):
-                block = quad * 4 + b
-                values = [st_ref[pl.ds(pl.multiple_of(f * LINES_PAD + block * 8, 8), 8), :] for f in range(3)]
-                for row in range(8):
-                    first = block * PLANE + group * 64 + row * 8
-                    plane = p_ref[pl.ds(pl.multiple_of(first, 8), 8), :]
-                    for f in range(3):
-                        sums[f * 8 + row] = sums[f * 8 + row] + plane * values[f]
-            return tuple(sums)
-
-        sums = lax.fori_loop(begin, end, degrees, (jnp.zeros((8, 128), F32),) * 24)
+
+    def degrees(quad, sums):
+        sums = list(sums)
+        for b in range(4):
+            block = quad * 4 + b
+            values = [st_ref[pl.ds(pl.multiple_of(f * LINES_PAD + block * 8, 8), 8), :] for f in range(3)]
+            for row in range(8):
+                first = block * PLANE + group * 64 + row * 8
+                plane = p_ref[pl.ds(pl.multiple_of(first, 8), 8), :]
+                for f in range(3):
+                    sums[f * 8 + row] = sums[f * 8 + row] + plane * values[f]
+        return tuple(sums)
+
+    zeros = (jnp.zeros((8, 128), F32),) * 24
+    sets = [lax.fori_loop(0, quads, degrees, zeros), lax.fori_loop(quads, QUADS, degrees, zeros)]
+    for which in range(2):
         for f in range(3):
-            parts = list(sums[f * 8 : f * 8 + 8])
+            north, south = fold_rows(sets[which][f * 8 : f * 8 + 8])
             line = which * 9 + f * 3
-            h_ref[pl.ds(n * 8 * MSG_C + line + s, 8, stride=MSG_C), :] = fold_rows(parts)
-            parts = [part * sign for part in parts]
-            h_ref[pl.ds((16 + n * 8) * MSG_C + line + 2 - s, 8, stride=MSG_C), :] = fold_rows(parts)
+            h_ref[pl.ds(n * 8 * MSG_C + line + s, 8, stride=MSG_C), :] = north
+            h_ref[pl.ds((16 + n * 8) * MSG_C + line + 2 - s, 8, stride=MSG_C), :] = south
 
 
 def inverse_operand(group, south, cp_ref, y_ref):
@@ -465,6 +466,7 @@
     p = lax.axis_index("lat")
     here = place_of(q)
     south = p >= LAT // 2
+    low_set = jnp.where(q < LON // 2, 2 * q, 63 - 2 * q)
     owned, half = q // 2, q % 2
     my_source = slot_of(p * 2 + half)
     back_mode = (q // 4 + 16 - p // 2 - p % 2 * 4) % 8 * 2 + q % 4 // 2
@@ -473,7 +475,7 @@
 
     zero_copy = pltpu.make_async_copy(zero_ref, ns_ref.at[:, :, 256:512], load_sem.at[8])
 
-    @pl.when(q >= 16)
+    @pl.when(q >= LON // 2)
     def _():
         zero_ref[...] = jnp.zeros_like(zero_ref)
         zero_copy.start()
@@ -514,7 +516,7 @@
             src_ref=source,
             dst_ref=target,
             send_sem=send_sem.at[stage],
-            recv_sem=recv_sem.at[4 if stage in (4, 5) else 5 if stage > 5 else stage, group],
+            recv_sem=recv_sem.at[stage, group],
             device_id=peer,
             device_id_type=MESH,
         )
@@ -575,67 +577,54 @@
                 (lon_of(place), p),
             )
 
-    def state_copies(index):
-        rows = pl.ds(index * HALF, HALF)
-        low = (
-            (2 * q + index, p),
-            lambda: copy(state_any.at[:, rows, :], low_state_ref, 4 + index, 0, (2 * q + index, p)),
-            lambda: pltpu.make_async_copy(state_any.at[:, rows, :], low_state_ref, recv_sem.at[4, 0]),
-        )
-        worker = 63 - 2 * q - index
-        high = (
-            (worker, p),
-            lambda: copy(state_any.at[:, rows, 0:256], high_state_ref, 4 + index, 1, (worker, p)),
-            lambda: pltpu.make_async_copy(state_any.at[:, rows, 0:256], high_state_ref, recv_sem.at[4, 1]),
-        )
-        return low, high
-
-    def new_copies():
-        low_rows = pl.ds(q % 2 * HALF, HALF)
-        high_rows = pl.ds((63 - q) % 2 * HALF, HALF)
-        owner = (63 - q) // 2
-        low = (
-            q // 2,
-            lambda: copy(low_new_ref, ns_ref.at[:, low_rows, :], 6, 0, (q // 2, p)),
-            lambda: pltpu.make_async_copy(low_new_ref, ns_ref.at[:, low_rows, :], recv_sem.at[5, 0]),
-        )
-        high = (
-            owner,
-            lambda: copy(high_new_ref, ns_ref.at[:, high_rows, 0:256], 7, 0, (owner, p)),
-            lambda: pltpu.make_async_copy(high_new_ref, ns_ref.at[:, high_rows, 0:256], recv_sem.at[5, 0]),
-        )
-        return low, high
-
-    def each_state_copy(act):
-        for index in range(2):
-            low, high = state_copies(index)
-            for (peer, remote, local), mine in ((low, q < 16), (high, q >= 16)):
-
-                @pl.when(jnp.logical_and(mine, peer[0] != q))
-                def _():
-                    act(remote, False)
-
-                @pl.when(jnp.logical_and(mine, peer[0] == q))
-                def _():
-                    act(local, True)
-
-    def each_new_copy(act):
-        for peer, remote, local in new_copies():
-
-            @pl.when(peer != q)
-            def _():
-                act(remote, False)
-
-            @pl.when(peer == q)
-            def _():
-                act(local, True)
-
-    def begin(item, own):
-        item().start()
-
-    def sent(item, own):
-        if not own:
-            item().wait_send()
+    partner = (LON - 1 - q, p)
+    keeps_low = q < LON // 2
+    mine, other = pl.ds(0, HALF), pl.ds(HALF, HALF)
+
+    def state_copies(low):
+        if low:
+            keep = pltpu.make_async_copy(state_any.at[:, mine, :], low_state_ref, recv_sem.at[4, 0])
+            return keep, copy(state_any.at[:, other, :], low_state_ref, 4, 0, partner)
+        keep = pltpu.make_async_copy(state_any.at[:, mine, 0:256], high_state_ref, recv_sem.at[4, 1])
+        return keep, copy(state_any.at[:, other, 0:256], high_state_ref, 4, 1, partner)
+
+    def new_copies(low):
+        if low:
+            keep = pltpu.make_async_copy(low_new_ref, ns_ref.at[:, mine, :], recv_sem.at[5, 1])
+            return keep, copy(high_new_ref, ns_ref.at[:, other, 0:256], 5, 0, partner)
+        keep = pltpu.make_async_copy(high_new_ref, ns_ref.at[:, mine, 0:256], recv_sem.at[5, 1])
+        return keep, copy(low_new_ref, ns_ref.at[:, other, :], 5, 0, partner)
+
+    def either(act):
+        @pl.when(keeps_low)
+        def _():
+            act(True)
+
+        @pl.when(jnp.logical_not(keeps_low))
+        def _():
+            act(False)
+
+    def send_state(low):
+        keep, go = state_copies(low)
+        keep.start()
+        go.start()
+
+    def send_new(low):
+        keep, go = new_copies(low)
+        keep.start()
+        go.start()
+
+    def sent_state(low):
+        state_copies(low)[1].wait_send()
+
+    def finish_new(low):
+        keep, go = new_copies(low)
+        keep.wait()
+        go.wait_send()
+        if not low:
+            zero_copy.wait()
+        part = ns_ref.at[:, other, :] if low else ns_ref.at[:, other, 0:256]
+        pltpu.make_async_copy(part, part, recv_sem.at[5, 0]).wait()
 
     loads[0].wait()
     gather_rows(t_ref, sb_ref)
@@ -652,8 +641,8 @@
     lax.fori_loop(1, LAT, tell, 0)
 
     loads[1].wait()
-    legendre_tables(q, start_ref, slope_ref, lag_ref, trig_ref, p_ref)
-    each_state_copy(begin)
+    legendre_tables(low_set, start_ref, slope_ref, lag_ref, trig_ref, p_ref)
+    either(send_state)
     fsum_ref[...] = jnp.zeros_like(fsum_ref)
     loads[2].wait()
     loads[3].wait()
@@ -676,12 +665,12 @@
         load.wait()
     wait(sb_ref, 0, (LON - 1) * MSG_G, send_sem.at[0])
     wait(g_ref, 0, 32 * MSG_C, recv_sem.at[1, 0])
-    analysis(q, g_ref, trig_ref, eo_ref, p_ref, a_ref)
-    each_state_copy(sent)
+    analysis(low_set, g_ref, trig_ref, eo_ref, p_ref, a_ref)
+    either(sent_state)
     pltpu.make_async_copy(low_state_ref, low_state_ref, recv_sem.at[4, 0]).wait()
     pltpu.make_async_copy(high_state_ref, high_state_ref, recv_sem.at[4, 1]).wait()
     update(
-        q,
+        low_set,
         stiff_ref[p],
         damp_ref[p],
         (low_state_ref, high_state_ref),
@@ -689,10 +678,10 @@
         (low_new_ref, high_new_ref),
         st_ref,
     )
-    each_new_copy(begin)
+    either(send_new)
 
     def synthesize(part, _):
-        lax.fori_loop(0, 3, lambda s, _: (synthesis(q, part * 3 + s, p_ref, st_ref, h_ref), 0)[1], 0)
+        lax.fori_loop(0, 3, lambda s, _: (synthesis(low_set, part * 3 + s, p_ref, st_ref, h_ref), 0)[1], 0)
         lax.fori_loop(0, 16, send_rows, part)
         return 0
 
@@ -718,18 +707,7 @@
     lax.fori_loop(0, 4, waves_group, 0)
     inverse_blocks(q, y_ref, ih_ref, il_ref, block_ref, w_ref, send_back)
     wait_sent(h_ref, back_mode == p, 2)
-    each_new_copy(sent)
-
-    @pl.when(q < 16)
-    def _():
-        pltpu.make_async_copy(ns_ref, ns_ref, recv_sem.at[5, 0]).wait()
-
-    @pl.when(q >= 16)
-    def _():
-        zero_copy.wait()
-        part = ns_ref.at[:, :, 0:256]
-        pltpu.make_async_copy(part, part, recv_sem.at[5, 0]).wait()
-
+    either(finish_new)
     wait(o_ref, 0, LON * MSG_G, recv_sem.at[3, 0])
     wait(w_ref, 0, (LON - 1) * MSG_G, send_sem.at[3])
 
@@ -788,7 +766,7 @@
             pltpu.VMEM((256, 2 * WAVES), BF16),
             pltpu.VMEM((rows, 128), F32),
             pltpu.SemaphoreType.DMA((9,)),
-            pltpu.SemaphoreType.DMA((8,)),
+            pltpu.SemaphoreType.DMA((6,)),
             pltpu.SemaphoreType.DMA((6, 4)),
             pltpu.SemaphoreType.REGULAR,
         ],

time: 77.7 us -> 75 us (0.965)
  the two profiles are of different devices: /device:TPU:129 before, /device:TPU:1 now
where the time goes in v4:
time: 75 us; the launch traced here: 74.8 us
  Pallas kernels  74.2 us (99%)
    pallas_call x1, Pallas kernels, body(): pl.pallas_call(kernel, out_shape=shapes, in_specs=[anywhere] * 9, out_spe...  72.2 us
    pallas_call x1, Pallas kernels, body(): pl.pallas_call(result_kernel, out_shape=shapes, in_specs=[vmem, vmem], ou...  1.96 us

profile of v4, /device:TPU:1, one launch (start us, length us, event | category | flops | bytes accessed | tf_op | source)
XLA Modules:
  0.0 74.8 jit_solution(2084694360355137696)
XLA Ops:
  0.6 72.2 %spectral_step.1 = (f32[6,16,512]{2,1,0:T(8,128)}, f32[864,128]{1,0:T(8,128)}) custom-call(f32[864,128]{1,0:T(8,128)} %bitcast.4, f32[6,16,512]{2,1,0:T(8,128)} %bitcast.5, f32[64,128]{1,0:T(8,128)} %constant.10.clone.start_any, f32[16]{0:T(128)} %stiff_any.1, f32[16]{0:T(128)} %damp_any.1, bf16[2048,1024]{1,0:T(8,128)(2,1)} %constant.11.clone.fh_any, ...), custom_call_target="tpu_custom_call" | custom-call | tf_op jit(solution)/shard_map/spectral_step/pallas_call | solution.py:731
  72.9 2.0 %results.1 = (f32[6,16,512]{2,1,0:T(8,128)}, f32[864,128]{1,0:T(8,128)}) custom-call(f32[6,16,512]{2,1,0:T(8,128)} %get-tuple-element.6.ns_ref, f32[864,128]{1,0:T(8,128)} %get-tuple-element.7.o_ref), custom_call_target="tpu_custom_call" | custom-call | tf_op jit(solution)/shard_map/results/pallas_call | solution.py:785

commit v5 on v4

--- a/solution.py
+++ b/solution.py
@@ -642,7 +642,6 @@
 
     loads[1].wait()
     legendre_tables(low_set, start_ref, slope_ref, lag_ref, trig_ref, p_ref)
-    either(send_state)
     fsum_ref[...] = jnp.zeros_like(fsum_ref)
     loads[2].wait()
     loads[3].wait()
@@ -661,6 +660,7 @@
     group = grid_group(3)
     pl.semaphore_wait(ready_sem, LAT - 1)
     forward_blocks(q, south, group, x_ref, fh_ref, fl_ref, fsum_ref, block_ref, m_ref, send_waves)
+    either(send_state)
     for load in loads[4:]:
         load.wait()
     wait(sb_ref, 0, (LON - 1) * MSG_G, send_sem.at[0])
@@ -678,7 +678,6 @@
         (low_new_ref, high_new_ref),
         st_ref,
     )
-    either(send_new)
 
     def synthesize(part, _):
         lax.fori_loop(0, 3, lambda s, _: (synthesis(low_set, part * 3 + s, p_ref, st_ref, h_ref), 0)[1], 0)
@@ -686,6 +685,7 @@
         return 0
 
     lax.fori_loop(0, 2, synthesize, 0)
+    either(send_new)
 
     def wait_sent(ref, own, stage):
         @pl.when(own)

time: 75 us -> 72.8 us (0.971)
  Pallas kernels: 74.2 us -> 72 us
    pallas_call x1, Pallas kernels: 72.2 us -> 70.1 us  [body(): pl.pallas_call(kernel, out_shape=shapes, in_specs=[anywhere] * 9, out_spe...]
where the time goes in v5:
time: 72.8 us; the launch traced here: 72.7 us
  Pallas kernels  72 us (99%)
    pallas_call x1, Pallas kernels, body(): pl.pallas_call(kernel, out_shape=shapes, in_specs=[anywhere] * 9, out_spe...  70.1 us
    pallas_call x1, Pallas kernels, body(): pl.pallas_call(result_kernel, out_shape=shapes, in_specs=[vmem, vmem], ou...  1.96 us

profile of v5, /device:TPU:1, one launch (start us, length us, event | category | flops | bytes accessed | tf_op | source)
XLA Modules:
  0.0 72.7 jit_solution(10194304446566329228)
XLA Ops:
  0.6 70.1 %spectral_step.1 = (f32[6,16,512]{2,1,0:T(8,128)}, f32[864,128]{1,0:T(8,128)}) custom-call(f32[864,128]{1,0:T(8,128)} %bitcast.4, f32[6,16,512]{2,1,0:T(8,128)} %bitcast.5, f32[64,128]{1,0:T(8,128)} %constant.10.clone.start_any, f32[16]{0:T(128)} %stiff_any.1, f32[16]{0:T(128)} %damp_any.1, bf16[2048,1024]{1,0:T(8,128)(2,1)} %constant.11.clone.fh_any, ...), custom_call_target="tpu_custom_call" | custom-call | tf_op jit(solution)/shard_map/spectral_step/pallas_call | solution.py:731
  70.7 2.0 %results.1 = (f32[6,16,512]{2,1,0:T(8,128)}, f32[864,128]{1,0:T(8,128)}) custom-call(f32[6,16,512]{2,1,0:T(8,128)} %get-tuple-element.6.ns_ref, f32[864,128]{1,0:T(8,128)} %get-tuple-element.7.o_ref), custom_call_target="tpu_custom_call" | custom-call | tf_op jit(solution)/shard_map/results/pallas_call | solution.py:785

commit v6 on v5

--- a/solution.py
+++ b/solution.py
@@ -712,15 +712,21 @@
     wait(w_ref, 0, (LON - 1) * MSG_G, send_sem.at[3])
 
 
-def result_kernel(ns_ref, o_ref, new_state_any, new_fields_any, sem):
-    copies = [
-        pltpu.make_async_copy(source, target, sem.at[index])
-        for index, (source, target) in enumerate(((ns_ref, new_state_any), (o_ref, new_fields_any)))
-    ]
-    for item in copies:
-        item.start()
-    for item in copies:
-        item.wait()
+def result_kernel(ns_any, o_any, new_state_any, new_fields_any, ns_ref, o_ref, in_sem, out_sem):
+    moves = []
+    for n in range(3):
+        part, rows = pl.ds(n * 2, 2), pl.ds(n * 288, 288)
+        moves.append((ns_any.at[part], ns_ref.at[part], new_state_any.at[part]))
+        moves.append((o_any.at[rows], o_ref.at[rows], new_fields_any.at[rows]))
+    loads = [pltpu.make_async_copy(a, b, in_sem.at[n]) for n, (a, b, _) in enumerate(moves)]
+    stores = [pltpu.make_async_copy(b, c, out_sem.at[n]) for n, (_, b, c) in enumerate(moves)]
+    for load in loads:
+        load.start()
+    for load, store in zip(loads, stores):
+        load.wait()
+        store.start()
+    for store in stores:
+        store.wait()
 
 
 def body(tendency, state, stiffness, damping):
@@ -785,9 +791,15 @@
     new_state, new_fields = pl.pallas_call(
         result_kernel,
         out_shape=shapes,
-        in_specs=[vmem, vmem],
+        in_specs=[anywhere, anywhere],
         out_specs=(anywhere, anywhere),
-        scratch_shapes=[pltpu.SemaphoreType.DMA((2,))],
+        scratch_shapes=[
+            pltpu.VMEM((FR, MDEV, WAVES), F32),
+            pltpu.VMEM((rows, 128), F32),
+            pltpu.SemaphoreType.DMA((6,)),
+            pltpu.SemaphoreType.DMA((6,)),
+        ],
+        compiler_params=pltpu.CompilerParams(vmem_limit_bytes=60 * 2**20),
         name="results",
     )(new_state, new_fields)
     return new_state.reshape(state.shape), new_fields.reshape(tendency.shape)

time: 72.8 us -> 72.8 us (level)
  no operation moved by 1% of the time
where the time goes in v6:
time: 72.8 us; the launch traced here: 72.6 us
  Pallas kernels  72 us (99%)
    pallas_call x1, Pallas kernels, body(): pl.pallas_call(kernel, out_shape=shapes, in_specs=[anywhere] * 9, out_spe...  70.1 us
    pallas_call x1, Pallas kernels, body(): pl.pallas_call(result_kernel, out_shape=shapes, in_specs=[anywhere, anywh...  1.92 us

profile of v6, /device:TPU:1, one launch (start us, length us, event | category | flops | bytes accessed | tf_op | source)
XLA Modules:
  0.0 72.6 jit_solution(17647049843584564494)
XLA Ops:
  0.6 70.1 %spectral_step.1 = (f32[6,16,512]{2,1,0:T(8,128)}, f32[864,128]{1,0:T(8,128)}) custom-call(f32[864,128]{1,0:T(8,128)} %bitcast.4, f32[6,16,512]{2,1,0:T(8,128)} %bitcast.5, f32[64,128]{1,0:T(8,128)} %constant.10.clone.start_any, f32[16]{0:T(128)} %stiff_any.1, f32[16]{0:T(128)} %damp_any.1, bf16[2048,1024]{1,0:T(8,128)(2,1)} %constant.11.clone.fh_any, ...), custom_call_target="tpu_custom_call" | custom-call | tf_op jit(solution)/shard_map/spectral_step/pallas_call | solution.py:737
  70.7 1.9 %results.1 = (f32[6,16,512]{2,1,0:T(8,128)}, f32[864,128]{1,0:T(8,128)}) custom-call(f32[6,16,512]{2,1,0:T(8,128)} %get-tuple-element.6.ns_any, f32[864,128]{1,0:T(8,128)} %get-tuple-element.7.o_any), custom_call_target="tpu_custom_call" | custom-call | tf_op jit(solution)/shard_map/results/pallas_call | solution.py:791
